TPU v7x, 32 devices: a whole 2x2x4 slice. The times are simulated.
32 devices in a mesh: parts: 2 (over x), pg: 4 (over z), tp: 4 (over y, core).
Axes of the slice: x: 2, y: 2, z: 4, core: 2. Of those that a mesh axis runs over, the one named last changes fastest.
Arguments:
- tokens: bfloat16 [32, 256, 8192], P(('parts', 'pg'), None, 'tp'), parts along dimension 0
- prefix_kv: bfloat16 [32, 512, 1024], P(('parts', 'pg'), None, 'tp'), parts along dimension 0
- counts: int32 [8], P('parts'), parts along dimension 0, may hold values from 0 to 4, as said below
- destinations: int32 [32], P('parts'), parts along dimension 0, may hold values from -1 to 7, as said below
- page_owner: int32 [128], P('parts'), parts along dimension 0, may hold values from 0 to 3, as said below
- prefix_len: int32 [32], P('parts'), parts along dimension 0, may hold values from 0 to 512, as said below
- ln_gain: bfloat16 [8192], replicated, may hold values from 0.099609375 to 1.8984375
- q_weight: bfloat16 [8192, 4096], P(None, 'tp'), may hold values from -0.0625 to 0.0625
- q_bias: bfloat16 [4096], P('tp'), may hold values from -3 to 3
- kv_weight: bfloat16 [8192, 1024], P(None, 'tp'), may hold values from -0.0625 to 0.0625
- kv_bias: bfloat16 [1024], P('tp'), may hold values from -3 to 3
- o_weight: bfloat16 [4096, 8192], P('tp'), may hold values from -0.09375 to 0.09375
Outputs:
- hidden: bfloat16 [16, 256, 8192], P(('parts', 'pg'), None, 'tp'), parts along dimension 0
- kv_pages: bfloat16 [128, 64, 1024], P(('parts', 'pg'), None, 'tp'), parts along dimension 0
There are 2 independent parts, one for each index of `parts`. A program takes and returns all parts, laid end to end along the dimension named above; an argument that names none is the same for every part. Nothing has to cross between parts.
Inputs may be any that keep to these rules, and one draw needn't show every extreme that they name: Group g holds counts[g] spans, in its first source slots; the counts sum to 8; some group holds 4 and some none. `destinations`: every held span names one work slot and every work slot is named by exactly one held span; span j < min(counts[g], 2) of group g names slot g * 2 + j; the other held spans name slots j >= counts[h] of groups h holding fewer than 2; slots holding no span hold -1. `page_owner`: no group owns more than 16 pages of held spans, and some group owns exactly 16; entries of slots holding no span are arbitrary. `prefix_len`: A multiple of 256.
All inputs are finite; a program needn't handle non-finite values.
Results may differ from a plain program's by a relative error of at most 0.0097.
Values may be sent and summed in bfloat16 or wider, within the bound.
No kernel may reach another device: no remote copies, remote signals or barrier semaphores. Data moves between devices by JAX's collectives and lax.ppermute only.
A program may use at most 192 MiB of HBM per device.

v0:
```python
import jax
import jax.numpy as jnp
from jax import lax
from jax.sharding import PartitionSpec as P

D = 8192
HQ = 32
KVH = 4
HD = 128
C = 256
PRE = 512
MAXW = 2
PAGE = 64
OWNCAP = 16


rope_base = 1000000.0
norm_eps = 1e-06


def work_sources(counts, destinations, groups):
    source_count = 2 * MAXW
    source_slot = jnp.arange(groups * source_count, dtype=jnp.int32)
    is_valid = source_slot % source_count < counts[source_slot // source_count]
    work_slot = jnp.arange(groups * MAXW, dtype=jnp.int32)
    matches = is_valid[None, :] & (destinations[None, :] == work_slot[:, None])
    source = jnp.sum(jnp.where(matches, source_slot[None, :], 0), axis=1)
    filled = jnp.any(matches, axis=1)
    return (source, filled, is_valid)


def page_ranks(is_valid, page_owner, groups):
    pages_per = C // PAGE
    page_valid = jnp.repeat(is_valid, pages_per)
    membership = (
        page_valid[:, None] & (page_owner[:, None] == jnp.arange(groups, dtype=jnp.int32)[None, :])
    ).astype(jnp.int32)
    earlier_count = jnp.cumsum(membership, axis=0) - membership
    return jnp.sum(earlier_count * membership, axis=1)


def rope_angles(positions):
    half_dim = HD // 2
    frequency = rope_base ** (-(jnp.arange(half_dim, dtype=jnp.float32) * (2.0 / HD)))
    angles = positions.astype(jnp.float32)[..., None] * frequency
    return (jnp.cos(angles), jnp.sin(angles))


def rotate(vectors, cosine, sine_table):
    half_dim = HD // 2
    first_half = vectors[..., :half_dim]
    second_half = vectors[..., half_dim:]
    return jnp.concatenate(
        [
            first_half * cosine - second_half * sine_table,
            second_half * cosine + first_half * sine_table,
        ],
        axis=-1,
    )


def head_block(rows, first_head, head_count):
    key_part = lax.dynamic_slice_in_dim(rows, first_head * HD, head_count * HD, 2)
    value_part = lax.dynamic_slice_in_dim(rows, KVH * HD + first_head * HD, head_count * HD, 2)
    return jnp.concatenate([key_part, value_part], axis=2)


def local(
    tokens,
    prefix_kv,
    counts,
    destinations,
    page_owner,
    prefix_len,
    ln_gain,
    q_weight,
    q_bias,
    kv_weight,
    kv_bias,
    o_weight,
):
    groups = lax.axis_size("pg")
    group_index = lax.axis_index("pg")
    column = lax.axis_index("tp")
    source_count = tokens.shape[0]
    heads_here = q_weight.shape[1] // HD
    group_size = HQ // KVH
    local_kv_heads = max(1, heads_here // group_size)
    first_kv_head = column * heads_here // group_size
    slice_width = prefix_kv.shape[2]
    extra_slots = source_count - MAXW
    source, filled, is_valid = work_sources(counts, destinations, groups)
    rank_table = page_ranks(is_valid, page_owner, groups)
    own_sources = lax.dynamic_slice_in_dim(source, group_index * MAXW, MAXW)
    stays_home = jnp.arange(MAXW, dtype=jnp.int32) < counts[group_index]
    spare_index = jnp.arange(groups * extra_slots, dtype=jnp.int32)
    spare_slot = spare_index // extra_slots * source_count + MAXW + spare_index % extra_slots
    spare_valid = MAXW + spare_index % extra_slots < counts[spare_index // extra_slots]
    wanted = group_index * MAXW + jnp.arange(MAXW, dtype=jnp.int32)
    matches = spare_valid[None, :] & (destinations[spare_slot][None, :] == wanted[:, None])
    chosen = jnp.sum(jnp.where(matches, spare_index[None, :], 0), axis=1)

    def settle(own_rows, moved_rows):
        return jnp.where(stays_home[:, None, None], own_rows, moved_rows[chosen])

    gathered = lax.all_gather(prefix_kv, "tp", axis=2, tiled=True)
    head_columns = head_block(gathered, first_kv_head, local_kv_heads)
    moved_tokens, moved_heads = (
        lax.all_gather(tokens[MAXW:], "pg", axis=0, tiled=True),
        lax.all_gather(head_columns[MAXW:], "pg", axis=0, tiled=True),
    )
    work_tokens = settle(tokens[:MAXW], moved_tokens)
    work_prefix = settle(head_columns[:MAXW], moved_heads)
    features = lax.all_gather(work_tokens, "tp", axis=2, tiled=True)
    feature_rows = features.astype(jnp.float32)
    inv_rms = lax.rsqrt(jnp.mean(feature_rows * feature_rows, axis=-1, keepdims=True) + norm_eps)
    normed = (feature_rows * inv_rms * ln_gain.astype(jnp.float32)).astype(jnp.bfloat16)
    flat_normed = normed.reshape(MAXW * C, D)
    queries = jnp.dot(flat_normed, q_weight, preferred_element_type=jnp.float32) + q_bias.astype(
        jnp.float32
    )
    fresh_columns = (
        jnp.dot(flat_normed, kv_weight, preferred_element_type=jnp.float32)
        + kv_bias.astype(jnp.float32)
    ).astype(jnp.bfloat16)
    fresh_all = lax.all_gather(
        fresh_columns.reshape(MAXW, C, slice_width), "tp", axis=2, tiled=True
    )
    prefix_start = prefix_len[own_sources]
    positions = prefix_start[:, None] + jnp.arange(C, dtype=jnp.int32)[None, :]
    cosine, sine_table = rope_angles(positions)
    cosine = cosine[:, :, None, :]
    sine_table = sine_table[:, :, None, :]
    queries = (
        rotate(queries.reshape(MAXW, C, heads_here, HD), cosine, sine_table) * HD ** (-0.5)
    ).astype(jnp.bfloat16)
    fresh_all = fresh_all.reshape(MAXW, C, 2, KVH, HD)
    new_keys = rotate(fresh_all[:, :, 0].astype(jnp.float32), cosine, sine_table).astype(
        jnp.bfloat16
    )
    new_kv = jnp.concatenate(
        [new_keys.reshape(MAXW, C, KVH * HD), fresh_all[:, :, 1].reshape(MAXW, C, KVH * HD)], axis=2
    )
    new_heads = head_block(new_kv, first_kv_head, local_kv_heads)
    all_rows = jnp.concatenate([work_prefix, new_heads], axis=1).reshape(
        MAXW, PRE + C, 2, local_kv_heads, HD
    )
    key_rows = all_rows[:, :, 0]
    value_rows = all_rows[:, :, 1]
    grouped = queries.reshape(MAXW, C, local_kv_heads, heads_here // local_kv_heads, HD)
    scores = jnp.einsum("wcngd,wlnd->wngcl", grouped, key_rows, preferred_element_type=jnp.float32)
    key_index = jnp.arange(PRE + C, dtype=jnp.int32)
    query_row = jnp.arange(C, dtype=jnp.int32)
    allowed = jnp.where(
        key_index[None, None, :] < PRE,
        key_index[None, None, :] < prefix_start[:, None, None],
        (key_index - PRE)[None, None, :] <= query_row[None, :, None],
    )
    scores = jnp.where(allowed[:, None, None], scores, -jnp.inf)
    row_max = jnp.max(scores, axis=-1, keepdims=True)
    weights = jnp.exp(scores - row_max)
    probabilities = (weights / jnp.sum(weights, axis=-1, keepdims=True)).astype(jnp.bfloat16)
    mixed_heads = jnp.einsum(
        "wngcl,wlnd->wcngd", probabilities, value_rows, preferred_element_type=jnp.float32
    ).astype(jnp.bfloat16)
    head_partial = jnp.dot(
        mixed_heads.reshape(MAXW * C, heads_here * HD), o_weight, preferred_element_type=jnp.float32
    ).reshape(MAXW, C, D)
    attended = lax.psum_scatter(
        head_partial.astype(jnp.bfloat16), "tp", scatter_dimension=2, tiled=True
    ).astype(jnp.float32)
    hidden = (work_tokens.astype(jnp.float32) + attended).astype(jnp.bfloat16)
    pages_per = C // PAGE
    own_columns = lax.dynamic_slice_in_dim(new_kv, column * slice_width, slice_width, 2)
    page_rows = own_columns.reshape(MAXW * pages_per, PAGE, slice_width)
    work_page = jnp.arange(groups * MAXW * pages_per, dtype=jnp.int32)
    source_page = source[work_page // pages_per] * pages_per + work_page % pages_per
    owner_of_page = page_owner[source_page]
    local_owner = lax.dynamic_slice_in_dim(
        owner_of_page, group_index * MAXW * pages_per, MAXW * pages_per
    )
    addressed = local_owner[None, :] == jnp.arange(groups, dtype=jnp.int32)[:, None]
    outbox = jnp.where(addressed[:, :, None, None], page_rows[None], jnp.zeros((), jnp.bfloat16))
    arrived = lax.all_to_all(outbox, "pg", split_axis=0, concat_axis=0, tiled=True).reshape(
        groups * MAXW * pages_per, PAGE, slice_width
    )
    retained = filled[work_page // pages_per] & (owner_of_page == group_index)
    slot_matches = retained[None, :] & (
        rank_table[source_page][None, :] == jnp.arange(OWNCAP, dtype=jnp.int32)[:, None]
    )
    slot_pick = jnp.sum(jnp.where(slot_matches, work_page[None, :], 0), axis=1)
    kv_pages = jnp.where(
        jnp.any(slot_matches, axis=1)[:, None, None],
        arrived[slot_pick],
        jnp.zeros((), jnp.bfloat16),
    )
    return (hidden, kv_pages)


def solution(mesh):
    in_specs = (
        P(("parts", "pg"), None, "tp"),
        P(("parts", "pg"), None, "tp"),
        P("parts"),
        P("parts"),
        P("parts"),
        P("parts"),
        P(),
        P(None, "tp"),
        P("tp"),
        P(None, "tp"),
        P("tp"),
        P("tp", None),
    )
    out_specs = (P(("parts", "pg"), None, "tp"), P(("parts", "pg"), None, "tp"))
    return jax.shard_map(local, mesh=mesh, in_specs=in_specs, out_specs=out_specs, check_vma=False)
```

profile of v0, /device:TPU:0, one launch (start us, length us, event | category | flops | bytes accessed | tf_op | source)
XLA Modules:
  0.0 468.8 jit_solution(8306757543559476620)
XLA Ops:
  7.2 0.7 all-gather.8.cloned.1.call-update
  8.0 3.2 slice.37
  11.2 36.1 %all-gather.8.cloned.1.call-done = bf16[4,512,1024]{2,1,0:T(8,128)(2,1)} async-done(((bf16[4,512,256]{2,1,0:T(8,128)(2,1)}), bf16[4,512,1024]{2,1,0:T(8,128)(2,1)}) %all-gather.8.cloned.1.call-update) | async-done | bytes 4194320 | tf_op jit(solution)/shard_map/all_gather | solution.py:106
  47.3 1.3 constant_dynamic-slice_fusion.4
  48.6 0.9 pad_maximum_fusion
  49.6 0.6 dynamic_slice.24
  50.2 0.6 gather_fusion
  50.9 0.6 gather_fusion.1
  51.5 0.6 iota_compare_fusion.7
  52.2 0.2 fusion.29
  52.4 146.7 %all-gather.6.cloned.1.call-done = bf16[8,256,2048]{2,1,0:T(8,128)(2,1)} async-done(((bf16[2,256,2048]{2,1,0:T(8,128)(2,1)}), bf16[8,256,2048]{2,1,0:T(8,128)(2,1)}) %all-gather.6.cloned.1.call-update) | async-done | bytes 8388624 | tf_op jit(solution)/shard_map/all_gather | solution.py:109
  199.1 4.1 gather_fusion.2
  203.2 3.4 slice_select_fusion
  206.7 0.7 gather_fusion.4
  207.5 0.1 select_reduce_fusion.2
  207.6 0.7 gather_fusion.7
  208.4 0.6 gather_fusion.5
  209.3 0.2 iota_compare_fusion
  209.4 1.0 multiply_cosine_fusion
  210.4 0.6 broadcast_select_fusion.1
  211.1 34.4 %all-gather.10.cloned.1.call-done = bf16[8,512,256]{2,1,0:T(8,128)(2,1)} async-done(((bf16[2,512,256]{2,1,0:T(8,128)(2,1)}), bf16[8,512,256]{2,1,0:T(8,128)(2,1)}) %all-gather.10.cloned.1.call-update) | async-done | bytes 2097168 | tf_op jit(solution)/shard_map/all_gather | solution.py:110
  245.5 2.2 gather_fusion.3
  247.7 1.1 fusion.21
  248.7 56.0 %all-gather.12.cloned.1.call-done = bf16[2,256,8192]{2,1,0:T(8,128)(2,1)} async-done(((bf16[2,256,2048]{2,1,0:T(8,128)(2,1)}), bf16[2,256,8192]{2,1,0:T(8,128)(2,1)}) %all-gather.12.cloned.1.call-update) | async-done | bytes 8388624 | tf_op jit(solution)/shard_map/all_gather | solution.py:114
  304.7 5.1 %fusion = f32[2,256]{1,0:T(2,128)S(1)} fusion(bf16[2,256,8192]{2,1,0:T(8,128)(2,1)} %all-gather.12.cloned.1.call-done), kind=kLoop, calls=%fused_computation.13 | loop fusion | flops 12582400 | bytes 8390656 | tf_op jit(solution)/shard_map/reduce_sum | solution.py:116
  309.8 9.9 %fusion.2 = bf16[2,256,8192]{2,1,0:T(8,128)(2,1)} fusion(bf16[2,256,8192]{2,1,0:T(8,128)(2,1)} %all-gather.12.cloned.1.call-done, f32[8192]{0:T(1024)S(1)} %convert_element_type.70, f32[2,256]{1,0:T(2,128)S(1)} %add_rsqrt_fusion), kind=kLoop, calls=%fused_computation.15 | loop fusion | flops 16777216 | bytes 16812032 | tf_op jit(solution)/shard_map/convert_element_type | solution.py:117
  319.7 7.6 %fusion.16 = bf16[512,256]{1,0:T(8,128)(2,1)} fusion(bf16[512,8192]{1,0:T(8,128)(2,1)} %bitcast.98, bf16[8192,256]{1,0:T(8,128)(2,1)} %param.21, f32[256]{0:T(256)S(1)} %convert_element_type.72), kind=kOutput, calls=%fused_computation.35 | convolution fusion | flops 2147745792 | bytes 12846080 | tf_op jit(solution)/shard_map/dot_general | solution.py:123
  327.3 0.2 reduce-scatter.2.cloned.1.call-start
  327.6 14.3 %add_bitcast_fusion = f32[64,8,8,128]{3,1,2,0:T(8,128)S(1)} fusion(bf16[512,8192]{1,0:T(8,128)(2,1)} %bitcast.99, bf16[8192,1024]{1,0:T(8,128)(2,1)} %param.19, f32[1024]{0:T(1024)S(1)} %convert_element_type.78), kind=kOutput, calls=%fused_computation.31 | convolution fusion | flops 8590458880 | bytes 27267072 | tf_op jit(solution)/shard_map/dot_general | solution.py:119
  341.9 0.5 copy.85
  342.3 0.7 fusion.45
  343.0 2.1 multiply_subtract_fusion
  345.1 2.6 reshape.454
  347.7 2.2 slice_bitcast_fusion
  349.9 2.0 reshape_squeeze.3
  351.9 1.9 subtract_convert_fusion
  353.8 0.7 pad_maximum_fusion.1
  354.6 0.2 convert_element_type.77
  354.8 1.1 constant_dynamic-update-slice_fusion
  356.0 0.9 copy-done.9
  356.9 1.1 maximum_maximum_fusion
  358.0 1.2 copy.68
  359.2 4.2 fusion.8
  363.5 2.2 fusion.9
  365.6 3.7 fusion.13
  369.4 17.0 %fusion.5 = bf16[2,256,8192]{2,1,0:T(8,128)(2,1)} fusion(bf16[2,256,1024]{1,2,0:T(8,128)(2,1)S(1)} %bitcast.105, bf16[1024,8192]{1,0:T(8,128)(2,1)} %param.23), kind=kOutput, calls=%fused_computation.21 | convolution fusion | flops 8594128896 | bytes 26214400 | tf_op jit(solution)/shard_map/dot_general | solution.py:166
  386.4 0.6 copy-done.3
  387.0 0.7 gather_fusion.8
  387.8 1.0 constant_dynamic-slice_fusion.2
  388.7 1.1 broadcast_select_fusion
  389.9 4.6 all-to-all-start
  394.5 0.1 fusion.28
  394.6 0.8 gather_fusion.6
  395.5 0.1 and.187
  395.7 0.1 reduce_window_sum.11
  395.8 0.2 select_reduce_fusion
  396.0 0.7 gather_fusion.9
  396.7 0.1 select_reduce_fusion.1
  396.8 0.1 fusion.26
  397.0 23.7 %all-to-all-done = bf16[4,8,64,256]{3,2,1,0:T(8,128)(2,1)S(1)} async-done(((bf16[4,8,64,256]{3,2,1,0:T(8,128)(2,1)}), bf16[4,8,64,256]{3,2,1,0:T(8,128)(2,1)S(1)}, u32[]{:S(2)}, u32[]{:S(2)}) %all-to-all-start) | async-done | bytes 1048608 | tf_op jit(solution)/shard_map/all_to_all | solution.py:184
  420.6 1.4 gather_fusion.10
  422.0 1.9 broadcast_select_fusion.2
  423.9 34.3 %reduce-scatter.2.cloned.1.call-done = bf16[2,256,2048]{2,1,0:T(8,128)(2,1)} async-done(((bf16[2,256,8192]{2,1,0:T(8,128)(2,1)}), bf16[2,256,2048]{2,1,0:T(8,128)(2,1)}) %reduce-scatter.2.cloned.1.call-update) | async-done | bytes 2097168 | tf_op jit(solution)/shard_map/reduce_scatter | solution.py:169
  458.2 3.7 add_convert_fusion
  (78 shorter events, 1.1 us)
Async XLA Ops:
  7.2 201.3 %copy-start = (s32[16]{0:T(128)S(1)}, s32[16]{0:T(128)}, u32[]{:S(2)}) copy-start(s32[16]{0:T(128)} %param.17) | copy-start | bytes 196
  7.2 40.1 %all-gather.8.cloned.1.call-start = ((), (), s32[]{:S(2)}) async-start(), calls=%async_computation.3 | async-start | bytes 5242880 | tf_op jit(solution)/shard_map/all_gather | solution.py:106
  7.9 191.2 %all-gather.6.cloned.1.call-start = ((), (), s32[]{:S(2)}) async-start(), calls=%async_computation.2 | async-start | bytes 10485760 | tf_op jit(solution)/shard_map/all_gather | solution.py:109
  11.1 38.4 %copy-start.2 = (s32[4]{0:T(128)S(1)}, s32[4]{0:T(128)}, u32[]{:S(2)}) copy-start(s32[4]{0:T(128)} %param.14) | copy-start | bytes 52
  11.1 39.7 %copy-start.4 = (s32[16]{0:T(128)S(1)}, s32[16]{0:T(128)}, u32[]{:S(2)}) copy-start(s32[16]{0:T(128)} %param.15) | copy-start | bytes 196
  11.2 234.3 %all-gather.10.cloned.1.call-start = ((), (), s32[]{:S(2)}) async-start(), calls=%async_computation.4 | async-start | bytes 2621440 | tf_op jit(solution)/shard_map/all_gather | solution.py:110
  49.5 255.2 %all-gather.12.cloned.1.call-start = ((), (), s32[]{:S(2)}) async-start(), calls=%async_computation.5 | async-start | bytes 10485760 | tf_op jit(solution)/shard_map/all_gather | solution.py:114
  52.2 154.4 %copy-start.12 = (pred[2]{0:T(512)(128)(4,1)}, pred[2]{0:T(512)(128)(4,1)S(1)}, u32[]{:S(2)}) copy-start(pred[2]{0:T(512)(128)(4,1)S(1)} %iota_compare_fusion.7) | copy-start | bytes 10
  203.2 3.5 copy-start.17
  203.2 4.2 copy-start.14
  203.2 4.2 copy-start.10
  206.6 41.0 %copy-start.13 = (pred[2]{0:T(512)(128)(4,1)S(1)}, pred[2]{0:T(512)(128)(4,1)}, u32[]{:S(2)}) copy-start(pred[2]{0:T(512)(128)(4,1)} %copy-done.12) | copy-start | bytes 10
  206.6 138.5 %all-gather.14.cloned.1.call-start = ((), (), s32[]{:S(2)}) async-start(), calls=%async_computation.6 | async-start | bytes 1310720 | tf_op jit(solution)/shard_map/all_gather | solution.py:126
  207.5 1.6 copy-start.11
  207.5 102.3 %copy-start.15 = (pred[16]{0:T(512)(128)(4,1)}, pred[16]{0:T(512)(128)(4,1)S(1)}, u32[]{:S(2)}) copy-start(pred[16]{0:T(512)(128)(4,1)S(1)} %fusion.32) | copy-start | bytes 52
  210.4 132.6 %copy-start.6 = (f32[2,256,64]{2,1,0:T(8,128)}, f32[2,256,64]{2,1,0:T(8,128)S(1)}, u32[]{:S(2)}) copy-start(f32[2,256,64]{2,1,0:T(8,128)S(1)} %get-tuple-element.14) | copy-start | bytes 393220
  210.4 132.6 %copy-start.7 = (f32[2,256,64]{2,1,0:T(8,128)}, f32[2,256,64]{2,1,0:T(8,128)S(1)}, u32[]{:S(2)}) copy-start(f32[2,256,64]{2,1,0:T(8,128)S(1)} %get-tuple-element.15) | copy-start | bytes 393220
  327.3 130.9 %reduce-scatter.2.cloned.1.call-start = ((), (), s32[]{:S(2)}) async-start(), calls=%async_computation.7 | async-start | bytes 10485760 | tf_op jit(solution)/shard_map/reduce_scatter | solution.py:169
  355.9 1.0 copy-start.9
  363.4 2.2 copy-start.8
  386.3 0.7 copy-start.3
  386.4 8.1 %copy-start.16 = (pred[16]{0:T(512)(128)(4,1)S(1)}, pred[16]{0:T(512)(128)(4,1)}, u32[]{:S(2)}) copy-start(pred[16]{0:T(512)(128)(4,1)} %copy-done.15) | copy-start | bytes 52
  386.4 71.9 %copy-start.5 = (bf16[2,256,2048]{2,1,0:T(8,128)(2,1)S(1)}, bf16[2,256,2048]{2,1,0:T(8,128)(2,1)}, u32[]{:S(2)}) copy-start(bf16[2,256,2048]{2,1,0:T(8,128)(2,1)} %slice_select_fusion) | copy-start | bytes 6291460
  389.9 30.8 %all-to-all-start = ((bf16[4,8,64,256]{3,2,1,0:T(8,128)(2,1)}), bf16[4,8,64,256]{3,2,1,0:T(8,128)(2,1)S(1)}, u32[]{:S(2)}, u32[]{:S(2)}) async-start(bf16[4,8,64,256]{3,2,1,0:T(8,128)(2,1)} %broadcast_select_fusion), calls=%async_computation.1 | async-start | bytes 2097152 | tf_op jit(solution)/shard_map/all_to_all | solution.py:184
  420.6 41.3 %copy-start.1 = (s32[16]{0:T(128)S(1)}, s32[16]{0:T(128)}, u32[]{:S(2)}) copy-start(s32[16]{0:T(128)} %param.17) | copy-start | bytes 196
Sparse Core Ops, SparseCore 0:
  9.6 37.7 all-gather.7
  49.5 149.6 all-gather.5
  201.3 44.1 all-gather.9
  247.5 57.2 all-gather.11
  327.4 16.8 all-gather.13
  386.5 71.7 reduce-scatter.1
where the time goes:
time: 470 us; the launch traced here: 469 us
  waiting for transfers between devices  332 us (71%)
  matrix products  46.8 us (10%)
  other arithmetic  41 us (9%)
  local copies, waits for them, and re-layouts  29.3 us (6%)
  between operations  14.6 us (3%)
  starting transfers between devices  5.03 us (1%)
    all_gather x1, waiting for transfers between devices, local(): lax.all_gather(tokens[MAXW:], 'pg', axis=0, tiled=True)  147 us
    all_gather x1, waiting for transfers between devices, local(): features = lax.all_gather(work_tokens, 'tp', axis=2, tiled=True)  56 us
    all_gather x1, waiting for transfers between devices, local(): gathered = lax.all_gather(prefix_kv, 'tp', axis=2, tiled=True)  36.1 us
    all_gather x1, waiting for transfers between devices, local(): lax.all_gather(head_columns[MAXW:], 'pg', axis=0, tiled=True)  34.4 us
    reduce_scatter x1, waiting for transfers between devices, local(): lax.psum_scatter(head_partial.astype(jnp.bfloat16), 'tp', scatter_dimensi...  34.3 us
    all_to_all x1, waiting for transfers between devices, local(): lax.all_to_all(outbox, 'pg', split_axis=0, concat_axis=0, tiled=True)  23.7 us
    dot_general x1, matrix products, local(): jnp.dot(mixed_heads.reshape(MAXW * C, heads_here * HD), o_weight, preferr...  17 us
    dot_general x1, matrix products, local(): jnp.dot(flat_normed, q_weight, preferred_element_type=jnp.float32)  14.3 us
  transfers between devices with their start and end apart: 7, of which 6 were waited for; matrix products, arithmetic and copies ran while one was open for 10% of the time, Pallas kernels for 0%

commit v1 on v0

--- a/solution.py
+++ b/solution.py
@@ -1,6 +1,12 @@
+import functools
+import itertools
+
 import jax
 import jax.numpy as jnp
+import numpy as np
 from jax import lax
+from jax.experimental import pallas as pl
+from jax.experimental.pallas import tpu as pltpu
 from jax.sharding import PartitionSpec as P
 
 D = 8192
@@ -65,7 +71,721 @@
     return jnp.concatenate([key_part, value_part], axis=2)
 
 
-def local(
+GROUPS = 4
+SHARD = D // KVH
+HEADS = HQ // KVH
+SLICE = 2 * HD
+HALF = C // 2
+NORM_ROWS = 16
+OUT_PARTS = 2
+ADD_PARTS = 4
+GROUP_PAIRS = [(a, b) for a in range(GROUPS) for b in range(GROUPS) if a != b]
+SMEM = pl.BlockSpec(memory_space=pltpu.SMEM)
+VMEM = pl.BlockSpec(memory_space=pltpu.VMEM)
+HBM = pl.BlockSpec(memory_space=pltpu.HBM)
+ANY = pl.BlockSpec(memory_space=pl.ANY)
+QUICK = pl.CostEstimate(flops=1, bytes_accessed=1, transcendentals=0)
+
+
+def kernel_params(mib):
+    return pltpu.CompilerParams(vmem_limit_bytes=mib * 2**20)
+
+
+def rows_of(*shape, dtype=jnp.bfloat16):
+    return jax.ShapeDtypeStruct(shape, dtype)
+
+
+def start_all(copies):
+    for copy in copies:
+        copy.start()
+    return copies
+
+
+def rope_tables():
+    frequency = rope_base ** (-(np.arange(HD // 2, dtype=np.float32) * np.float32(2.0 / HD)))
+    positions = np.arange(PRE + C, dtype=np.float32)
+    angles = positions[:, None] * frequency.astype(np.float32)
+    cosine, sine = np.cos(angles), np.sin(angles)
+    tables = (np.concatenate([cosine, cosine], 1), np.concatenate([-sine, sine], 1))
+    return [jnp.asarray(t.astype(np.float32).reshape(-1, C, HD)) for t in tables]
+
+
+def round_patterns():
+    double = []
+    for senders in itertools.combinations(range(GROUPS), 2):
+        low, high = [g for g in range(GROUPS) if g not in senders]
+        double.append([(senders[0], low), (senders[1], high)])
+        double.append([(senders[0], high), (senders[1], low)])
+    return [[pair] for pair in GROUP_PAIRS] + double
+
+
+def leave_copies(slot, tokens_ref, prefix_ref, leave_ref, sems):
+    return [
+        pltpu.make_async_copy(tokens_ref.at[slot], leave_ref.at[:, pl.ds(0, SHARD)], sems.at[0])
+    ] + [
+        pltpu.make_async_copy(
+            prefix_ref.at[slot, pl.ds(half * C, C)],
+            leave_ref.at[:, pl.ds(SHARD + half * SLICE, SLICE)],
+            sems.at[1 + half],
+        )
+        for half in range(2)
+    ]
+
+
+def route_kernel(
+    group_ref, counts_ref, destinations_ref, prefix_len_ref, tokens_ref, prefix_ref,
+    plan_ref, first_ref, second_ref, leave_first, leave_second, table_ref, sems,
+):
+    group = group_ref[0]
+    counts = [counts_ref[g] for g in range(GROUPS)]
+
+    def pick(flags, default):
+        found = jnp.int32(default)
+        for g in reversed(range(GROUPS)):
+            found = jnp.where(flags[g], g, found)
+        return found
+
+    full = pick([count == 2 * MAXW for count in counts], 0)
+    other = pick([(counts[g] > MAXW) & (full != g) for g in range(GROUPS)], -1)
+    other_group = jnp.maximum(other, 0)
+    other_spare = jnp.where(other >= 0, counts_ref[other_group] - MAXW, 0)
+    full_to = [destinations_ref[full * 4 + 2 + i] for i in range(2)]
+    other_to = [destinations_ref[other_group * 4 + 2 + i] for i in range(2)]
+    clash_first = (other_spare > 0) & (full_to[0] // MAXW == other_to[0] // MAXW)
+    clash_second = (other_spare > 1) & (full_to[1] // MAXW == other_to[1] // MAXW)
+    swapped = clash_first | clash_second
+    moves, copies = [], []
+    for r in range(2):
+        a, b = full, full_to[r] // MAXW
+        take = jnp.where(swapped, 1 - r, r)
+        second = other_spare > take
+        to = jnp.where(swapped, other_to[1 - r], other_to[r])
+        c, d = other_group, to // MAXW
+        single_index = a * 3 + b - (b > a).astype(jnp.int32)
+        low, high = jnp.minimum(a, c), jnp.maximum(a, c)
+        low_to = jnp.where(a < c, b, d)
+        high_to = jnp.where(a < c, d, b)
+        pair = jnp.where(low == 0, 0, jnp.where(low == 1, 3, 5)) + high - low - 1
+        double_index = 12 + 2 * pair + (low_to > high_to).astype(jnp.int32)
+        (first_ref, second_ref)[r][0] = jnp.where(second, double_index, single_index)
+        leaving = jnp.where((group == c) & second, 2 + take, 2 + r)
+        leave_ref = (leave_first, leave_second)[r]
+        copies += start_all(leave_copies(leaving, tokens_ref, prefix_ref, leave_ref, sems.at[r]))
+        moves.append((a, b, full_to[r], 2 + r, second, c, d, to, 2 + take))
+    for g in range(GROUPS):
+        got, slots, origins = [], [], []
+        for a, b, a_to, a_slot, second, c, d, c_to, c_slot in moves:
+            from_full = b == g
+            got.append(from_full | (second & (d == g)))
+            slots.append(jnp.where(from_full, a_to, c_to) % MAXW)
+            origins.append(jnp.where(from_full, a * 4 + a_slot, c * 4 + c_slot))
+        for r in range(2):
+            home_slot = jnp.where(got[1 - r], 1 - slots[1 - r], r)
+            slot = jnp.where(got[r], slots[r], home_slot)
+            table_ref[g * 8 + r] = jnp.where(got[r], 0, 1)
+            table_ref[g * 8 + 2 + r] = slot
+            table_ref[g * 8 + 4 + r] = prefix_len_ref[jnp.where(got[r], origins[r], g * 4 + slot)]
+            if r == 0:
+                plan_ref[8 + g] = slot
+    for i in range(6):
+        plan_ref[i] = table_ref[group * 8 + i]
+    for copy in copies:
+        copy.wait()
+
+
+def route(group, counts, destinations, prefix_len, tokens, prefix_kv):
+    leaving = rows_of(C, SHARD + 2 * SLICE)
+    one = rows_of(1, dtype=jnp.int32)
+    return pl.pallas_call(
+        route_kernel,
+        out_shape=(rows_of(16, dtype=jnp.int32), one, one, leaving, leaving),
+        in_specs=[SMEM] * 4 + [ANY] * 2,
+        out_specs=(SMEM, SMEM, SMEM, VMEM, VMEM),
+        scratch_shapes=[
+            pltpu.SMEM((GROUPS * 8,), jnp.int32),
+            pltpu.SemaphoreType.DMA((2, 3)),
+        ],
+        cost_estimate=QUICK,
+        name="route",
+    )(group, counts, destinations, prefix_len, tokens, prefix_kv)
+
+
+def settle_kernel(
+    r, column_ref, plan_ref, tokens_ref, prefix_ref, arrived_ref, rows_ref, mine_ref, other_ref, *refs
+):
+    halves_of_rows, sems = refs[:-1], refs[-1]
+    at_home = plan_ref[r] == 1
+    slot = plan_ref[2 + r]
+    odd = column_ref[0] % 2
+    halves = [(half, part) for half in range(PRE // C) for part in range(2)]
+
+    def token_copies(source):
+        whole = [pltpu.make_async_copy(source, rows_ref, sems.at[0])]
+        return whole + [
+            pltpu.make_async_copy(source.at[pl.ds(half * HALF, HALF)], ref, sems.at[5 + half])
+            for half, ref in enumerate(halves_of_rows)
+        ]
+
+    def head(half, part):
+        target = (mine_ref, other_ref)[part].at[pl.ds(half * C, C)]
+        side = pl.multiple_of(jnp.where(odd == part, 0, HD), HD)
+        return target, side
+
+    @pl.when(at_home)
+    def _():
+        start_all(token_copies(tokens_ref.at[slot]))
+        for i, (half, part) in enumerate(halves):
+            target, side = head(half, part)
+            source = prefix_ref.at[slot, pl.ds(half * C, C), pl.ds(side, HD)]
+            pltpu.make_async_copy(source, target, sems.at[1 + i]).start()
+
+    moved = token_copies(arrived_ref.at[:, pl.ds(0, SHARD)])
+    for i, (half, part) in enumerate(halves):
+        target, side = head(half, part)
+        place = pl.multiple_of(SHARD + half * SLICE + side, HD)
+        source = arrived_ref.at[:, pl.ds(place, HD)]
+        moved.append(pltpu.make_async_copy(source, target, sems.at[1 + i]))
+
+    @pl.when(jnp.logical_not(at_home))
+    def _():
+        start_all(moved)
+
+    for copy in moved:
+        copy.wait()
+
+
+def settle(r, column, plan, tokens, prefix_kv, arrived):
+    return pl.pallas_call(
+        functools.partial(settle_kernel, r),
+        out_shape=(rows_of(C, SHARD), rows_of(PRE, HD), rows_of(PRE, HD))
+        + (rows_of(HALF, SHARD),) * (2 * r),
+        in_specs=[SMEM] * 2 + [ANY] * 3,
+        out_specs=(VMEM,) * (3 + 2 * r),
+        scratch_shapes=[pltpu.SemaphoreType.DMA((3 + 2 * (PRE // C),))],
+        cost_estimate=QUICK,
+        name=f"settle_{r}",
+    )(column, plan, tokens, prefix_kv, arrived)
+
+
+def turn(block, cosine, sine):
+    return block * cosine + pltpu.roll(block, HD // 2, 1) * sine
+
+
+def table_copies(r, plan_ref, tables, held_ref, sems):
+    block = plan_ref[4 + r] // C
+    return [
+        pltpu.make_async_copy(table.at[block], held_ref.at[i], sems.at[i])
+        for i, table in enumerate(tables)
+    ]
+
+
+def fresh_kernel(r, split, column_ref, plan_ref, gain_ref, bias_ref, *refs):
+    pieces, refs = refs[: sum(split)], refs[sum(split) :]
+    cos_ref, sin_ref, weight_ref, normed_ref, fresh_ref, mine_ref, other_ref = refs[:7]
+    held_ref, turn_ref, sems, turn_sems = refs[7:]
+    column = column_ref[0]
+    copies = start_all(
+        [pltpu.make_async_copy(weight_ref.at[k], held_ref.at[k], sems.at[k]) for k in range(KVH)]
+    )
+    turns = start_all(table_copies(r, plan_ref, (cos_ref, sin_ref), turn_ref, turn_sems))
+
+    for half in range(2):
+        sources, at = [], 0
+        for parts in split:
+            sources.append((pieces[at + half], 0) if parts == 2 else (pieces[at], half * HALF))
+            at += parts
+
+        def rows(i, carry):
+            start = i * NORM_ROWS
+            blocks = [
+                (ref, pl.ds(pl.multiple_of(first + start, NORM_ROWS), NORM_ROWS))
+                for ref, first in sources
+            ]
+            total = jnp.zeros((NORM_ROWS, HD), jnp.float32)
+            for ref, here in blocks:
+                for j in range(SHARD // HD):
+                    x = ref[here, j * HD : (j + 1) * HD].astype(jnp.float32)
+                    total += x * x
+            inv_rms = lax.rsqrt(jnp.sum(total, axis=1, keepdims=True) * (1.0 / D) + norm_eps)
+            there = pl.ds(pl.multiple_of(half * HALF + start, NORM_ROWS), NORM_ROWS)
+            for k, (ref, here) in enumerate(blocks):
+                owner = column ^ k
+                x = ref[here, :].astype(jnp.float32)
+                normed_ref[owner, there, :] = (x * inv_rms * gain_ref[owner]).astype(jnp.bfloat16)
+            return carry
+
+        lax.fori_loop(0, HALF // NORM_ROWS, rows, 0, unroll=4)
+    terms = []
+    for k in range(KVH):
+        copies[k].wait()
+        terms.append(jnp.dot(normed_ref[k], held_ref[k], preferred_element_type=jnp.float32))
+    total = (terms[0] + terms[1]) + (terms[2] + terms[3])
+    fresh = (total + bias_ref[...].astype(jnp.float32)).astype(jnp.bfloat16)
+    for copy in turns:
+        copy.wait()
+    is_key = column < KVH // 2
+    blocks = []
+    for h in range(2):
+        block = fresh[:, h * HD : (h + 1) * HD]
+        turned = turn(block.astype(jnp.float32), turn_ref[0], turn_ref[1]).astype(jnp.bfloat16)
+        blocks.append(jnp.where(is_key, turned, block))
+        fresh_ref[:, h * HD : (h + 1) * HD] = blocks[h]
+    odd = column % 2 == 1
+    mine_ref[...] = jnp.where(odd, blocks[1], blocks[0])
+    other_ref[...] = jnp.where(odd, blocks[0], blocks[1])
+
+
+def fresh_rows(r, column, plan, pieces, gain, kv_weight, kv_bias, tables):
+    flat = [part for piece in pieces for part in piece]
+    head = rows_of(C, HD)
+    return pl.pallas_call(
+        functools.partial(fresh_kernel, r, [len(piece) for piece in pieces]),
+        out_shape=(rows_of(KVH, C, SHARD), rows_of(C, SLICE), head, head),
+        in_specs=[SMEM] * 2 + [VMEM] * (2 + len(flat)) + [HBM] * 3,
+        out_specs=(VMEM,) * 4,
+        scratch_shapes=[
+            pltpu.VMEM((KVH, SHARD, SLICE), jnp.bfloat16),
+            pltpu.VMEM((2, C, HD), jnp.float32),
+            pltpu.SemaphoreType.DMA((KVH,)),
+            pltpu.SemaphoreType.DMA((2,)),
+        ],
+        compiler_params=kernel_params(16),
+        cost_estimate=QUICK,
+        name=f"fresh_{r}",
+    )(column, plan, gain, kv_bias, *flat, *tables, kv_weight)
+
+
+def query_kernel(
+    r, plan_ref, normed_ref, bias_ref, cos_ref, sin_ref, weight_ref,
+    out_ref, held_ref, total_ref, turn_ref, sems, turn_sems,
+):
+    depth = SHARD // 2
+    start_all(
+        [
+            pltpu.make_async_copy(
+                weight_ref.at[i // 2, pl.ds(i % 2 * depth, depth)], held_ref.at[i], sems.at[i]
+            )
+            for i in range(2 * KVH)
+        ]
+    )
+    turns = start_all(table_copies(r, plan_ref, (cos_ref, sin_ref), turn_ref, turn_sems))
+    total_ref[...] = jnp.broadcast_to(bias_ref[...].astype(jnp.float32), total_ref.shape)
+
+    def add_term(i, carry):
+        pltpu.make_async_copy(held_ref.at[i], held_ref.at[i], sems.at[i]).wait()
+        here = pl.ds(pl.multiple_of(i % 2 * depth, depth), depth)
+        total_ref[...] += jnp.dot(
+            normed_ref[i // 2, :, here], held_ref[i], preferred_element_type=jnp.float32
+        )
+        return carry
+
+    lax.fori_loop(0, 2 * KVH, add_term, 0)
+    for copy in turns:
+        copy.wait()
+    for h in range(HEADS):
+        here = slice(h * HD, (h + 1) * HD)
+        block = turn(total_ref[:, here], turn_ref[0], turn_ref[1])
+        out_ref[:, here] = (block * HD ** (-0.5)).astype(jnp.bfloat16)
+
+
+def query_rows(r, plan, normed, q_weight, q_bias, tables):
+    columns = HEADS * HD
+    return pl.pallas_call(
+        functools.partial(query_kernel, r),
+        out_shape=rows_of(C, columns),
+        in_specs=[SMEM] + [VMEM] * 2 + [HBM] * 3,
+        out_specs=VMEM,
+        scratch_shapes=[
+            pltpu.VMEM((2 * KVH, SHARD // 2, columns), jnp.bfloat16),
+            pltpu.VMEM((C, columns), jnp.float32),
+            pltpu.VMEM((2, C, HD), jnp.float32),
+            pltpu.SemaphoreType.DMA((2 * KVH,)),
+            pltpu.SemaphoreType.DMA((2,)),
+        ],
+        compiler_params=kernel_params(24),
+        cost_estimate=QUICK,
+        name=f"queries_{r}",
+    )(plan, normed, q_bias, *tables, q_weight)
+
+
+def weight_copies(weight_ref, held_ref, block, sems):
+    width = SHARD // OUT_PARTS
+    return [
+        pltpu.make_async_copy(
+            weight_ref.at[:, pl.ds(pl.multiple_of(block * SHARD + i * width, width), width)],
+            held_ref.at[:, pl.ds(i * width, width)],
+            sems.at[i],
+        )
+        for i in range(OUT_PARTS)
+    ]
+
+
+def multiply_out(rows_ref, held_ref, sems, addends, *outs):
+    width = SHARD // OUT_PARTS
+
+    def part(i, carry):
+        here = pl.ds(pl.multiple_of(i * width, width), width)
+        pltpu.make_async_copy(held_ref.at[:, here], held_ref.at[:, here], sems.at[i]).wait()
+        total = jnp.dot(rows_ref[...], held_ref[:, here], preferred_element_type=jnp.float32)
+        for ref in addends:
+            total += ref[:, here].astype(jnp.float32)
+        for k, ref in enumerate(outs):
+            height = ref.shape[0]
+            ref[:, here] = total[k * height : (k + 1) * height].astype(ref.dtype)
+        return carry
+
+    lax.fori_loop(0, OUT_PARTS, part, 0)
+
+
+def attend_kernel(r, steps, parts, column_ref, plan_ref, query_ref, *refs):
+    old_kept, old_crossed, new_kept, new_crossed, weight_ref, heads_ref = refs[:6]
+    outs, (held_ref, keys_ref, values_ref, sems) = refs[6:-4], refs[-4:]
+    column = column_ref[0]
+    for i, step in enumerate(steps):
+        start_all(weight_copies(weight_ref, held_ref.at[i], column ^ step, sems.at[i]))
+    upper = column >= KVH // 2
+    for rows, kept, crossed in ((pl.ds(0, PRE), old_kept, old_crossed), (pl.ds(PRE, C), new_kept, new_crossed)):
+        keys_ref[rows, :] = jnp.where(upper, crossed[...], kept[...])
+        values_ref[rows, :] = jnp.where(upper, kept[...], crossed[...])
+    seen = [
+        jnp.where(plan_ref[4 + r] > i * C, 0.0, -jnp.inf).astype(jnp.float32)
+        for i in range(PRE // C)
+    ]
+    causal = lax.broadcasted_iota(jnp.int32, (C, C), 1) <= lax.broadcasted_iota(
+        jnp.int32, (C, C), 0
+    )
+    key_blocks = range(PRE // C + 1)
+
+    def score(h):
+        query = query_ref[:, h * HD : (h + 1) * HD]
+        scores = lax.dot_general(
+            query, keys_ref[...], (((1,), (1,)), ((), ())), preferred_element_type=jnp.float32
+        )
+        return [scores[:, i * C : (i + 1) * C] for i in key_blocks]
+
+    upcoming = score(0)
+    for h in range(HEADS):
+        blocks = upcoming
+        if h + 1 < HEADS:
+            upcoming = score(h + 1)
+        blocks = [block + bias for block, bias in zip(blocks, seen)] + [
+            jnp.where(causal, blocks[-1], -jnp.inf)
+        ]
+        top = jnp.max(functools.reduce(jnp.maximum, blocks), axis=1, keepdims=True)
+        blocks = [jnp.exp(block - top) for block in blocks]
+        share = 1.0 / jnp.sum(functools.reduce(jnp.add, blocks), axis=1, keepdims=True)
+        mixed = jnp.zeros((C, HD), jnp.float32)
+        for i in key_blocks:
+            mixed += jnp.dot(
+                blocks[i].astype(jnp.bfloat16),
+                values_ref[i * C : (i + 1) * C, :],
+                preferred_element_type=jnp.float32,
+            )
+        heads_ref[:, h * HD : (h + 1) * HD] = (mixed * share).astype(jnp.bfloat16)
+    multiply_out(heads_ref, held_ref.at[0], sems.at[0], (), *outs[:parts])
+    for i, out_ref in enumerate(outs[parts:], 1):
+        multiply_out(heads_ref, held_ref.at[i], sems.at[i], (), out_ref)
+
+
+def attend(r, column, plan, queries, old, new, o_weight, steps, parts):
+    columns = HEADS * HD
+    return pl.pallas_call(
+        functools.partial(attend_kernel, r, steps, parts),
+        out_shape=(rows_of(C, columns),)
+        + (rows_of(C // parts, SHARD),) * parts
+        + (rows_of(C, SHARD),) * (len(steps) - 1),
+        in_specs=[SMEM] * 2 + [VMEM] * 5 + [HBM],
+        out_specs=(VMEM,) * (parts + len(steps)),
+        scratch_shapes=[
+            pltpu.VMEM((len(steps), columns, SHARD), jnp.bfloat16),
+            pltpu.VMEM((PRE + C, HD), jnp.bfloat16),
+            pltpu.VMEM((PRE + C, HD), jnp.bfloat16),
+            pltpu.SemaphoreType.DMA((len(steps), OUT_PARTS)),
+        ],
+        compiler_params=kernel_params(10 + 4 * len(steps)),
+        cost_estimate=pl.CostEstimate(
+            flops=4 * C * (PRE + C) * columns + 2 * len(steps) * C * columns * SHARD,
+            bytes_accessed=(2 + 5 * len(steps)) * 2**20,
+            transcendentals=C * (PRE + C) * HEADS,
+        ),
+        name=f"attend_{r}",
+    )(column, plan, queries, *old, *new, o_weight)
+
+
+def output_kernel(steps, column_ref, heads_ref, weight_ref, *refs):
+    outs, (held_ref, sems) = refs[-2 - len(steps) : -2], refs[-2:]
+    addends = refs[: -2 - len(steps)]
+    for i, step in enumerate(steps):
+        start_all(weight_copies(weight_ref, held_ref.at[i], column_ref[0] ^ step, sems.at[i]))
+    for i, out_ref in enumerate(outs):
+        multiply_out(heads_ref, held_ref.at[i], sems.at[i], addends, out_ref)
+
+
+def output_blocks(column, heads, o_weight, steps, addends=(), dtype=jnp.bfloat16):
+    return pl.pallas_call(
+        functools.partial(output_kernel, steps),
+        out_shape=(rows_of(C, SHARD, dtype=dtype),) * len(steps),
+        in_specs=[SMEM, VMEM, HBM] + [VMEM] * len(addends),
+        out_specs=(VMEM,) * len(steps),
+        scratch_shapes=[
+            pltpu.VMEM((len(steps), HEADS * HD, SHARD), jnp.bfloat16),
+            pltpu.SemaphoreType.DMA((len(steps), OUT_PARTS)),
+        ],
+        compiler_params=kernel_params(8 + 4 * len(steps)),
+        cost_estimate=QUICK,
+        name="output_" + "".join(map(str, steps)),
+    )(column, heads, o_weight, *addends)
+
+
+def add_kernel(across_ref, *refs):
+    parts, outs = refs[:ADD_PARTS], refs[ADD_PARTS:]
+    height = C // ADD_PARTS
+    for i, ref in enumerate(parts):
+        rows = slice(i * height, (i + 1) * height)
+        total = across_ref[rows, :].astype(jnp.float32) + ref[...].astype(jnp.float32)
+        first = i * height % outs[0].shape[0]
+        out_ref = outs[i * height // outs[0].shape[0]]
+        out_ref[first : first + height, :] = total.astype(jnp.bfloat16)
+
+
+def add_parts(across, parts, pieces):
+    return pl.pallas_call(
+        add_kernel,
+        out_shape=(rows_of(C // pieces, SHARD),) * pieces,
+        in_specs=[VMEM] * (1 + len(parts)),
+        out_specs=(VMEM,) * pieces,
+        compiler_params=kernel_params(8),
+        cost_estimate=QUICK,
+        name="add",
+    )(across, *parts)
+
+
+def finish_kernel(r, whole, split, plan_ref, *refs):
+    held_ref, sems = refs[-2:]
+    out_ref = refs[-3]
+    slot = plan_ref[2 + r]
+    copies = []
+    for half in range(2):
+        here = slice(half * HALF, (half + 1) * HALF)
+        total = sum(ref[here, :].astype(jnp.float32) for ref in refs[:whole])
+        for ref in refs[whole : whole + split * (half + 1)][split * half :]:
+            total += ref[...].astype(jnp.float32)
+        held_ref[here, :] = total.astype(jnp.bfloat16)
+        copies += start_all(
+            [
+                pltpu.make_async_copy(
+                    held_ref.at[pl.ds(half * HALF, HALF)],
+                    out_ref.at[slot, pl.ds(half * HALF, HALF)],
+                    sems.at[half],
+                )
+            ]
+        )
+    for copy in copies:
+        copy.wait()
+
+
+def finish(r, plan, addends, halves, hidden):
+    earlier = [] if hidden is None else [hidden]
+    operands = (plan, *addends, *halves, *earlier)
+    return pl.pallas_call(
+        functools.partial(finish_kernel, r, len(addends), len(halves) // 2),
+        out_shape=rows_of(MAXW, C, SHARD),
+        in_specs=[SMEM] + [VMEM] * (len(addends) + len(halves)) + [ANY] * len(earlier),
+        out_specs=ANY,
+        scratch_shapes=[pltpu.VMEM((C, SHARD), jnp.bfloat16), pltpu.SemaphoreType.DMA((2,))],
+        input_output_aliases={len(operands) - 1: 0} if earlier else {},
+        compiler_params=kernel_params(8),
+        cost_estimate=QUICK,
+        name=f"finish_{r}",
+    )(*operands)
+
+
+def pages_kernel(group_ref, counts_ref, destinations_ref, owner_ref, plan_ref, *refs):
+    sources, (out_ref, held_ref, filled_ref, sems) = refs[:-4], refs[-4:]
+    copies = start_all(
+        [
+            pltpu.make_async_copy(source, held_ref.at[i], sems.at[i])
+            for i, source in enumerate(sources)
+        ]
+    )
+    out_ref[...] = jnp.zeros(out_ref.shape, out_ref.dtype)
+    filled_ref[0] = 0
+    group = group_ref[0]
+    for copy in copies:
+        copy.wait()
+
+    def span(s, carry):
+        @pl.when(s % (2 * MAXW) < counts_ref[s // (2 * MAXW)])
+        def _():
+            target = destinations_ref[s]
+            holder = target // MAXW
+            place = jnp.where(plan_ref[8 + holder] == target % MAXW, 0, 1)
+            away = jnp.where(group < holder, group - holder + GROUPS, group - holder)
+            for i in range(C // PAGE):
+                @pl.when(owner_ref[s * (C // PAGE) + i] == group)
+                def _():
+                    rank = filled_ref[0]
+                    filled_ref[0] = rank + 1
+                    out_ref[jnp.minimum(rank, OWNCAP - 1)] = held_ref[
+                        away, place, i * PAGE : (i + 1) * PAGE, :
+                    ]
+
+        return carry
+
+    lax.fori_loop(0, GROUPS * 2 * MAXW, span, 0)
+
+
+def place_pages(group, counts, destinations, page_owner, plan, gathered):
+    return pl.pallas_call(
+        pages_kernel,
+        out_shape=rows_of(OWNCAP, PAGE, SLICE),
+        in_specs=[SMEM] * 5 + [ANY] * len(gathered),
+        out_specs=VMEM,
+        scratch_shapes=[
+            pltpu.VMEM((GROUPS, 2, C, SLICE), jnp.bfloat16),
+            pltpu.SMEM((1,), jnp.int32),
+            pltpu.SemaphoreType.DMA((GROUPS,)),
+        ],
+        cost_estimate=QUICK,
+        name="pages",
+    )(group, counts, destinations, page_owner, plan, *gathered)
+
+
+def stay(weight):
+    return pltpu.with_memory_space_constraint(weight, pltpu.HBM)
+
+
+def after(rows, other):
+    return lax.optimization_barrier((rows, other))[0]
+
+
+def routed_layer(
+    tokens,
+    prefix_kv,
+    counts,
+    destinations,
+    page_owner,
+    prefix_len,
+    ln_gain,
+    q_weight,
+    q_bias,
+    kv_weight,
+    kv_bias,
+    o_weight,
+):
+    group = lax.axis_index("pg").reshape(1)
+    column = lax.axis_index("tp")
+    columns = column.reshape(1)
+    plan, *choices, leave_first, leave_second = route(
+        group, counts, destinations, prefix_len, tokens, prefix_kv
+    )
+    gain = ln_gain.astype(jnp.float32).reshape(KVH, 1, SHARD)
+    q_blocks = stay(q_weight.reshape(KVH, SHARD, HEADS * HD))
+    kv_blocks = stay(kv_weight.reshape(KVH, SHARD, SLICE))
+    o_weight = stay(o_weight)
+    q_row, kv_row = q_bias.reshape(1, -1), kv_bias.reshape(1, -1)
+    tables = [stay(table) for table in rope_tables()]
+    keeps_own = (column == 0) | (column == KVH - 1)
+
+    def swap(rows, step):
+        return lax.ppermute(rows, "tp", [(i, i ^ step) for i in range(KVH)])
+
+    def share_head(mine, other):
+        passed = swap(other, 1)
+        return jnp.where(keeps_own, mine, passed), jnp.where(keeps_own, passed, mine)
+
+    def rotate_groups(rows):
+        return [
+            lax.ppermute(rows, "pg", [(i, (i + step) % GROUPS) for i in range(GROUPS)])
+            for step in range(1, GROUPS)
+        ]
+
+    def add_pair(a, b):
+        return (a.astype(jnp.float32) + b.astype(jnp.float32)).astype(jnp.bfloat16)
+
+    def first_round(pairs, leaving):
+        return lax.ppermute(leaving, "pg", pairs)
+
+    def second_round(pairs, leaving, rows):
+        across = swap(rows, 2)
+        return lax.ppermute(leaving, "pg", pairs), swap(rows, 1), across, swap(across, 1)
+
+    patterns = round_patterns()
+    arrived = lax.switch(
+        choices[0][0], [functools.partial(first_round, pairs) for pairs in patterns], leave_first
+    )
+    rows_0, *old_0 = settle(0, columns, plan, tokens, prefix_kv, arrived)
+    leave_second, rows_0 = lax.optimization_barrier((leave_second, rows_0))
+    arrived, *others_0 = lax.switch(
+        choices[1][0],
+        [functools.partial(second_round, pairs) for pairs in patterns],
+        leave_second,
+        rows_0,
+    )
+    rows_1, *old_1, top_rows_1, bottom_rows_1 = settle(
+        1, columns, plan, tokens, prefix_kv, arrived
+    )
+    others_0, old_0, rows_1 = lax.optimization_barrier((others_0, old_0, rows_1))
+
+    beside_1 = swap(rows_1, 1)
+    top_1 = swap(top_rows_1, 2)
+    old_kept_0, old_crossing_0 = share_head(*old_0)
+    pieces = [[rows_0]] + [[rows] for rows in others_0]
+    normed, fresh_0, *new_0 = fresh_rows(
+        0, columns, plan, pieces, gain, kv_blocks, kv_row, tables
+    )
+    new_kept_0, new_crossing_0 = share_head(*new_0)
+    old_crossed_0 = swap(after(old_crossing_0, fresh_0), 2)
+    new_crossed_0 = swap(new_crossing_0, 2)
+    queries = query_rows(0, plan, after(normed, beside_1), q_blocks, q_row, tables)
+    bottom_1 = swap(after(bottom_rows_1, queries), 2)
+    old_kept_1, old_crossing_1 = share_head(*old_1)
+    old_crossed_1 = swap(after(old_crossing_1, fresh_0), 2)
+    _, *corner, beside_0, across, kept_0 = attend(
+        0, columns, plan, after(queries, (top_1, old_crossed_1)), (old_kept_0, old_crossed_0),
+        (new_kept_0, new_crossed_0), o_weight, (3, 1, 2, 0), ADD_PARTS,
+    )
+    corner = [swap(rows, 1) for rows in after(corner, bottom_1)]
+    sum_top, sum_bottom = add_parts(across, corner, 2)
+    total_top = swap(sum_top, 2)
+    passed_0 = swap(beside_0, 1)
+
+    pieces = [[after(rows_1, sum_top)], [beside_1], [top_1, bottom_1]]
+    pieces.append([swap(rows, 1) for rows in pieces[2]])
+    normed, fresh_1, *new_1 = fresh_rows(
+        1, columns, plan, pieces, gain, kv_blocks, kv_row, tables
+    )
+    new_kept_1, new_crossing_1 = share_head(*new_1)
+    new_crossed_1 = swap(new_crossing_1, 2)
+    queries = query_rows(1, plan, after(normed, passed_0), q_blocks, q_row, tables)
+    heads, *corner = attend(
+        1, columns, plan, after(queries, total_top), (old_kept_1, old_crossed_1),
+        (new_kept_1, new_crossed_1), o_weight, (3,), ADD_PARTS,
+    )
+    total_bottom = swap(after(sum_bottom, heads), 2)
+    corner = [swap(rows, 1) for rows in corner]
+    across, beside_1 = output_blocks(columns, heads, o_weight, (2, 1))
+    (sum_all,) = add_parts(across, corner, 1)
+    sum_all = after(sum_all, total_bottom)
+    total_1 = swap(sum_all, 2)
+
+    fresh = jnp.stack([fresh_0, after(fresh_1, sum_all)])
+    gathered = [fresh] + rotate_groups(fresh)
+    passed_1 = swap(after(beside_1, sum_all), 1)
+    (base_1,) = output_blocks(
+        columns, after(heads, sum_all), o_weight, (0,), (rows_1, passed_1), jnp.float32
+    )
+    hidden = finish(
+        0, plan, (rows_0, kept_0, after(passed_0, sum_all)), (total_top, total_bottom), None
+    )
+    hidden = finish(1, plan, (base_1, total_1), (), hidden)
+    kv_pages = place_pages(
+        group, counts, destinations, page_owner, plan, after(gathered, hidden)
+    )
+    return (hidden, kv_pages)
+
+
+def gathered_layer(
     tokens,
     prefix_kv,
     counts,
@@ -213,4 +933,8 @@
         P("tp", None),
     )
     out_specs = (P(("parts", "pg"), None, "tp"), P(("parts", "pg"), None, "tp"))
-    return jax.shard_map(local, mesh=mesh, in_specs=in_specs, out_specs=out_specs, check_vma=False)
+    if mesh.shape["pg"] == 4 and mesh.shape["tp"] == KVH:
+        layer = routed_layer
+    else:
+        layer = gathered_layer
+    return jax.shard_map(layer, mesh=mesh, in_specs=in_specs, out_specs=out_specs, check_vma=False)

time: 470 us -> 247 us (0.53)
  waiting for transfers between devices: 332 us -> 84.8 us
  starting transfers between devices: 5.03 us -> 89.9 us
  Pallas kernels: 0 us -> 65.2 us
  matrix products: 46.8 us -> 0 us
  other arithmetic: 41 us -> 0.11 us
  local copies, waits for them, and re-layouts: 29.3 us -> 5.69 us
  between operations: 14.6 us -> 2.5 us
    all_gather x5 -> x0, waiting for transfers between devices: 273 us -> none  [the longest x1 147 us: local(): lax.all_gather(tokens[MAXW:], 'pg', axis=0, tiled=True)]
    ppermute x0 -> x34, starting transfers between devices: none -> 89.9 us  [the longest x3 64.5 us: rotate_groups(): lax.ppermute(rows, 'pg', [(i, (i + step) % GROUPS) for i in range(GROUPS)])]
    ppermute x0 -> x34, waiting for transfers between devices: none -> 84.8 us  [the longest x29 32.8 us: swap(): return lax.ppermute(rows, 'tp', [(i, i ^ step) for i in range(KVH)])]
    pallas_call x0 -> x16, Pallas kernels: none -> 65.2 us  [the longest x2 16.5 us: query_rows(): pl.pallas_call(functools.partial(query_kernel, r), out_shape=rows_of(C, c...]
    dot_general x5 -> x0, matrix products: 46.8 us -> none  [the longest x1 17 us: local(): jnp.dot(mixed_heads.reshape(MAXW * C, heads_here * HD), o_weight, preferr...]
    reduce_scatter x1 -> x0, waiting for transfers between devices: 34.3 us -> none  [local(): lax.psum_scatter(head_partial.astype(jnp.bfloat16), 'tp', scatter_dimensi...]
    all_to_all x1 -> x0, waiting for transfers between devices: 23.7 us -> none  [local(): lax.all_to_all(outbox, 'pg', split_axis=0, concat_axis=0, tiled=True)]
    convert_element_type x7 -> x0, other arithmetic: 13.7 us -> none  [the longest x1 9.86 us: local(): (feature_rows * inv_rms * ln_gain.astype(jnp.float32)).astype(jnp.bfloat16)]
  transfers between devices with their start and end apart: 7 -> 34, of which waited for: 6 -> 11; matrix products, arithmetic and copies ran while one was open for 10% -> 0% of each run, Pallas kernels for 0% -> 19%
where the time goes in v1:
time: 247 us; the launch traced here: 248 us
  starting transfers between devices  89.9 us (36%)
  waiting for transfers between devices  84.8 us (34%)
  Pallas kernels  65.2 us (26%)
  local copies, waits for them, and re-layouts  5.69 us (2%)
  between operations  2.5 us (1%)
    ppermute x3, starting transfers between devices, rotate_groups(): lax.ppermute(rows, 'pg', [(i, (i + step) % GROUPS) for i in range(GROUPS)])  64.5 us
    ppermute x29, waiting for transfers between devices, swap(): return lax.ppermute(rows, 'tp', [(i, i ^ step) for i in range(KVH)])  32.8 us
    ppermute x1, waiting for transfers between devices, first_round(): return lax.ppermute(leaving, 'pg', pairs)  26.9 us
    pallas_call x2, Pallas kernels, query_rows(): pl.pallas_call(functools.partial(query_kernel, r), out_shape=rows_of(C, c...  16.5 us
    ppermute x3, waiting for transfers between devices, rotate_groups(): lax.ppermute(rows, 'pg', [(i, (i + step) % GROUPS) for i in range(GROUPS)])  15.3 us
    pallas_call x2, Pallas kernels, attend(): pl.pallas_call(functools.partial(attend_kernel, r, steps, parts), out_sha...  13.8 us
    ppermute x29, starting transfers between devices, swap(): return lax.ppermute(rows, 'tp', [(i, i ^ step) for i in range(KVH)])  12.8 us
    pallas_call x2, Pallas kernels, fresh_rows(): pl.pallas_call(functools.partial(fresh_kernel, r, [len(piece) for piece i...  11.1 us
  transfers between devices with their start and end apart: 34, of which 11 were waited for; matrix products, arithmetic and copies ran while one was open for 0% of the time, Pallas kernels for 19%

profile of v1, /device:TPU:0, one launch (start us, length us, event | category | flops | bytes accessed | tf_op | source)
XLA Modules:
  0.0 248.2 jit_solution(10247003725677419808)
XLA Ops:
  0.6 3.0 %route.1 = (s32[16]{0:T(128)}, s32[1]{0:T(128)}, s32[1]{0:T(128)}, bf16[256,2560]{1,0:T(8,128)(2,1)S(1)}, bf16[256,2560]{1,0:T(8,128)(2,1)S(1)}) custom-call(s32[1]{0:T(128)} %bitcast.group_ref, s32[4]{0:T(128)} %counts_ref.3, s32[16]{0:T(128)} %destinations_ref.3, s32[16]{0:T(128)} %prefix_len_ref.1, bf16[4,256,2048]{2,1,0:T(8,128)(2,1)} %tokens_ref.5, ...), custom_call_target="tpu_custom_call" | custom-call | flops 1 | bytes 1 | tf_op jit(solution)/shard_map/route/pallas_call | solution.py:199
  4.9 33.0 %conditional.2 = (bf16[256,2560]{1,0:T(8,128)(2,1)}) conditional(s32[]{:T(128)} %bitcast.4, bf16[256,2560]{1,0:T(8,128)(2,1)S(1)} %get-tuple-element.269, bf16[256,2560]{1,0:T(8,128)(2,1)S(1)} %get-tuple-element.269, bf16[256,2560]{1,0:T(8,128)(2,1)S(1)} %get-tuple-element.269, ...), branch_computations={%region_0.0_spmd, %region_1.0_spmd, %region_2.0_spmd, %region_3.0_... | conditional | bytes 5242928 | solution.py:714
  5.0 6.0 %collective-permute-start.16 = (bf16[256,2560]{1,0:T(8,128)(2,1)S(1)}, bf16[256,2560]{1,0:T(8,128)(2,1)}, u32[]{:S(2)}, u32[]{:S(2)}) collective-permute-start(bf16[256,2560]{1,0:T(8,128)(2,1)S(1)} %param.16), channel_id=1, source_target_pairs={{0,4},{12,8},{1,5},{13,9},{2,6},{14,10},{3,7},{15,11},{16,20},{28,... | collective-permute-start | bytes 3932168 | tf_op jit(solution)/shard_map/cond/branch_16_fun/ppermute | solution.py:707
  11.0 26.9 %collective-permute-done.16 = bf16[256,2560]{1,0:T(8,128)(2,1)} collective-permute-done((bf16[256,2560]{1,0:T(8,128)(2,1)S(1)}, bf16[256,2560]{1,0:T(8,128)(2,1)}, u32[]{:S(2)}, u32[]{:S(2)}) %collective-permute-start.16) | collective-permute-done | bytes 1310752 | tf_op jit(solution)/shard_map/cond/branch_16_fun/ppermute | solution.py:707
  37.9 2.7 %settle_0.1 = (bf16[256,2048]{1,0:T(8,128)(2,1)S(1)}, bf16[512,128]{1,0:T(8,128)(2,1)}, bf16[512,128]{1,0:T(8,128)(2,1)}) custom-call(s32[1]{0:T(128)} %bitcast.1.column_ref, s32[16]{0:T(128)} %get-tuple-element.265.plan_ref, bf16[4,256,2048]{2,1,0:T(8,128)(2,1)} %tokens_ref.5, bf16[4,512,256]{2,1,0:T(8,128)(2,1)} %prefix_ref.5, ...), custom_call_target="tpu_custom_call" | custom-call | flops 1 | bytes 1 | tf_op jit(solution)/shard_map/settle_0/pallas_call | solution.py:258
  40.6 34.0 %conditional.3 = (bf16[256,2560]{1,0:T(8,128)(2,1)}, bf16[256,2048]{1,0:T(8,128)(2,1)}, bf16[256,2048]{1,0:T(8,128)(2,1)}, bf16[256,2048]{1,0:T(8,128)(2,1)}) conditional(s32[]{:T(128)} %bitcast.3, (bf16[256,2560]{1,0:T(8,128)(2,1)S(1)}, bf16[256,2048]{1,0:T(8,128)(2,1)S(1)}) %tuple.170, ...), branch_computations={%region_24.0_spmd, %region_25.0_spmd, %region_26.0_spmd, %region_2... | conditional | bytes 17825984 | solution.py:719
  40.6 1.6 collective-permute-start.30
  42.2 6.6 %collective-permute-start.28 = (bf16[256,2560]{1,0:T(8,128)(2,1)S(1)}, bf16[256,2560]{1,0:T(8,128)(2,1)}, u32[]{:S(2)}, u32[]{:S(2)}) collective-permute-start(bf16[256,2560]{1,0:T(8,128)(2,1)S(1)} %get-tuple-element.147), channel_id=1, source_target_pairs={{0,8},{1,9},{2,10},{3,11},{16,24},{17,25},{18,26},{19,27}} | collective-permute-start | bytes 3932168 | tf_op jit(solution)/shard_map/cond/branch_1_fun/ppermute | solution.py:711
  48.8 16.0 %collective-permute-done.30 = bf16[256,2048]{1,0:T(8,128)(2,1)} collective-permute-done((bf16[256,2048]{1,0:T(8,128)(2,1)S(1)}, bf16[256,2048]{1,0:T(8,128)(2,1)}, u32[]{:S(2)}, u32[]{:S(2)}) %collective-permute-start.30) | collective-permute-done | bytes 1048608 | tf_op jit(solution)/shard_map/cond/branch_1_fun/ppermute | solution.py:691
  64.8 0.0 collective-permute-start.31
  64.8 0.0 collective-permute-done.29
  64.8 9.8 %collective-permute-done.28 = bf16[256,2560]{1,0:T(8,128)(2,1)} collective-permute-done((bf16[256,2560]{1,0:T(8,128)(2,1)S(1)}, bf16[256,2560]{1,0:T(8,128)(2,1)}, u32[]{:S(2)}, u32[]{:S(2)}) %collective-permute-start.28) | collective-permute-done | bytes 1310752 | tf_op jit(solution)/shard_map/cond/branch_1_fun/ppermute | solution.py:711
  74.6 3.8 %settle_1.1 = (bf16[256,2048]{1,0:T(8,128)(2,1)}, bf16[512,128]{1,0:T(8,128)(2,1)}, bf16[512,128]{1,0:T(8,128)(2,1)}, bf16[128,2048]{1,0:T(8,128)(2,1)}, bf16[128,2048]{1,0:T(8,128)(2,1)}) custom-call(s32[1]{0:T(128)} %bitcast.1.column_ref, s32[16]{0:T(128)} %get-tuple-element.265.plan_ref, bf16[4,256,2048]{2,1,0:T(8,128)(2,1)} %tokens_ref.5, ...), custom_call_target="tpu_custom_call" | custom-call | flops 1 | bytes 1 | tf_op jit(solution)/shard_map/settle_1/pallas_call | solution.py:258
  78.4 0.1 collective-permute-start.120
  78.5 0.5 collective-permute-start.124
  79.0 0.1 collective-permute-start.122
  79.1 0.5 collective-permute-start.121
  79.6 6.3 %fresh_0.1 = (bf16[4,256,2048]{2,1,0:T(8,128)(2,1)S(1)}, bf16[256,256]{1,0:T(8,128)(2,1)S(1)}, bf16[256,128]{1,0:T(8,128)(2,1)S(1)}, bf16[256,128]{1,0:T(8,128)(2,1)S(1)}) custom-call(s32[1]{0:T(128)} %bitcast.1.column_ref, s32[16]{0:T(128)S(1)} %copy-done.3, f32[4,1,2048]{2,1,0:T(1,128)S(1)} %bitcast.9, bf16[1,256]{1,0:T(2,128)(2,1)S(1)} %reshape.37.bias_ref, ...), custom_call_target="tpu_custom_call" | custom-call | flops 1 | bytes 1 | tf_op jit(solution)/shard_map/fresh_0/pallas_call | solution.py:341
  86.0 2.1 copy-done.1
  88.0 0.2 collective-permute-start.126
  88.3 1.6 collective-permute-start.123
  89.9 0.5 collective-permute-start.125
  90.4 1.6 collective-permute-start.127
  92.0 2.2 copy-done.2
  94.2 8.3 %queries_0.1.query_ref = bf16[256,1024]{1,0:T(8,128)(2,1)S(1)} custom-call(s32[16]{0:T(128)S(1)} %copy-done.3, bf16[4,256,2048]{2,1,0:T(8,128)(2,1)S(1)} %copy-done.2, bf16[1,1024]{1,0:T(2,128)(2,1)S(1)} %reshape.39.bias_ref, f32[3,256,128]{2,1,0:T(8,128)} %constant.22.clone.refs_4_.cos_ref.refs_6_, f32[3,256,128]{2,1,0:T(8,128)} %constant.23.clone.refs_5_.sin_ref.refs_7_, ...), custom_call_target="tpu_custom_call" | custom-call | flops 1 | bytes 1 | tf_op jit(solution)/shard_map/queries_0/pallas_call | solution.py:393
  102.5 0.6 collective-permute-start.128
  103.1 9.1 %attend_0.1 = (bf16[256,1024]{1,0:T(8,128)(2,1)}, bf16[64,2048]{1,0:T(8,128)(2,1)S(1)}, bf16[64,2048]{1,0:T(8,128)(2,1)S(1)}, bf16[64,2048]{1,0:T(8,128)(2,1)S(1...) custom-call(s32[1]{0:T(128)} %bitcast.1.column_ref, ...), custom_call_target="tpu_custom_call" | custom-call | flops 5100273664 | bytes 23068672 | tf_op jit(solution)/shard_map/attend_0/pallas_call | solution.py:492
  112.2 0.0 copy-start
  112.2 3.7 %collective-permute-done.128.refs_3_ = bf16[128,2048]{1,0:T(8,128)(2,1)S(1)} collective-permute-done((bf16[128,2048]{1,0:T(8,128)(2,1)S(1)}, bf16[128,2048]{1,0:T(8,128)(2,1)S(1)}, u32[]{:S(2)}, u32[]{:S(2)}) %collective-permute-start.128) | collective-permute-done | bytes 524320 | tf_op jit(solution)/shard_map/ppermute | solution.py:691
  115.9 0.5 collective-permute-start.135
  116.4 0.0 collective-permute-start.130
  116.4 0.5 collective-permute-start.133
  116.9 0.0 collective-permute-start.134
  116.9 0.5 collective-permute-done.129.refs_0_
  117.4 0.1 collective-permute-start.131
  117.5 1.7 collective-permute-done.130.refs_1_
  119.3 0.1 collective-permute-start.132
  119.4 1.7 collective-permute-done.131.refs_2_
  121.1 0.4 collective-permute-done.132.refs_3_
  121.5 0.2 add.2
  121.8 0.6 collective-permute-start.136
  122.3 4.8 %fresh_1.1 = (bf16[4,256,2048]{2,1,0:T(8,128)(2,1)S(1)}, bf16[256,256]{1,0:T(8,128)(2,1)S(1)}, bf16[256,128]{1,0:T(8,128)(2,1)S(1)}, bf16[256,128]{1,0:T(8,128)(2,1)S(1)}) custom-call(s32[1]{0:T(128)} %bitcast.1.column_ref, s32[16]{0:T(128)S(1)} %copy-done.3, f32[4,1,2048]{2,1,0:T(1,128)S(1)} %bitcast.10, bf16[1,256]{1,0:T(2,128)(2,1)S(1)} %reshape.37.bias_ref, ...), custom_call_target="tpu_custom_call" | custom-call | flops 1 | bytes 1 | tf_op jit(solution)/shard_map/fresh_1/pallas_call | solution.py:341
  127.1 0.1 collective-permute-start.137
  127.2 1.2 collective-permute-done.137
  128.5 1.6 collective-permute-start.138
  130.1 8.3 %queries_1.1.query_ref = bf16[256,1024]{1,0:T(8,128)(2,1)S(1)} custom-call(s32[16]{0:T(128)S(1)} %copy-done.3, bf16[4,256,2048]{2,1,0:T(8,128)(2,1)S(1)} %get-tuple-element.311.normed_ref, bf16[1,1024]{1,0:T(2,128)(2,1)S(1)} %reshape.39.bias_ref, f32[3,256,128]{2,1,0:T(8,128)} %constant.22.clone.refs_4_.cos_ref.refs_6_, ...), custom_call_target="tpu_custom_call" | custom-call | flops 1 | bytes 1 | tf_op jit(solution)/shard_map/queries_1/pallas_call | solution.py:393
  138.4 4.7 %attend_1.1 = (bf16[256,1024]{1,0:T(8,128)(2,1)S(1)}, bf16[64,2048]{1,0:T(8,128)(2,1)S(1)}, bf16[64,2048]{1,0:T(8,128)(2,1)S(1)}, bf16[64,2048]{1,0:T(8,128)(2,1)S(1)}, bf16[64,2048]{1,0:T(8,128)(2,1)S(1)}) custom-call(s32[1]{0:T(128)} %bitcast.1.column_ref, s32[16]{0:T(128)S(1)} %copy-done.3, bf16[256,1024]{1,0:T(8,128)(2,1)S(1)} %queries_1.1.query_ref, ...), custom_call_target="tpu_custom_call" | custom-call | flops 1879048192 | bytes 7340032 | tf_op jit(solution)/shard_map/attend_1/pallas_call | solution.py:492
  143.1 0.6 collective-permute-start.143
  143.7 0.5 collective-permute-start.140
  144.2 0.5 collective-permute-start.142
  144.7 4.5 %output_21.1 = (bf16[256,2048]{1,0:T(8,128)(2,1)S(1)}, bf16[256,2048]{1,0:T(8,128)(2,1)S(1)}) custom-call(s32[1]{0:T(128)} %bitcast.1.column_ref, bf16[256,1024]{1,0:T(8,128)(2,1)S(1)} %get-tuple-element.324.heads_ref, bf16[1024,8192]{1,0:T(8,128)(2,1)} %weight_ref.3), custom_call_target="tpu_custom_call" | custom-call | flops 1 | bytes 1 | tf_op jit(solution)/shard_map/output_21/pallas_call | solution.py:525
  149.2 0.2 add.3
  149.5 7.4 %collective-permute-done.143.refs_4_ = bf16[128,2048]{1,0:T(8,128)(2,1)S(1)} collective-permute-done((bf16[128,2048]{1,0:T(8,128)(2,1)S(1)}, bf16[128,2048]{1,0:T(8,128)(2,1)S(1)}, u32[]{:S(2)}, u32[]{:S(2)}) %collective-permute-start.143) | collective-permute-done | bytes 524320 | tf_op jit(solution)/shard_map/ppermute | solution.py:691
  156.9 0.5 collective-permute-start.145
  157.4 60.2 %collective-permute-start.148 = (bf16[2,256,256]{2,1,0:T(8,128)(2,1)S(1)}, bf16[2,256,256]{2,1,0:T(8,128)(2,1)S(1)}, u32[]{:S(2)}, u32[]{:S(2)}) collective-permute-start(bf16[2,256,256]{2,1,0:T(8,128)(2,1)S(1)} %pad_maximum_fusion.refs_0_), channel_id=1, source_target_pairs={{0,12},{4,0},{8,4},{12,8},{1,13},{5,1},{9,5},{13,9},{2,14},{6,2},{... | collective-permute-start | bytes 786440 | tf_op jit(solution)/shard_map/ppermute | solution.py:699
  217.6 2.8 %collective-permute-start.147 = (bf16[2,256,256]{2,1,0:T(8,128)(2,1)S(1)}, bf16[2,256,256]{2,1,0:T(8,128)(2,1)S(1)}, u32[]{:S(2)}, u32[]{:S(2)}) collective-permute-start(bf16[2,256,256]{2,1,0:T(8,128)(2,1)S(1)} %pad_maximum_fusion.refs_0_), channel_id=1, source_target_pairs={{0,8},{4,12},{8,0},{12,4},{1,9},{5,13},{9,1},{13,5},{2,10},{6,14},... | collective-permute-start | bytes 786440 | tf_op jit(solution)/shard_map/ppermute | solution.py:699
  220.4 1.5 collective-permute-start.146
  221.9 1.9 finish_0.1.refs_2_
  223.9 3.1 %output_0.1.refs_0_ = f32[256,2048]{1,0:T(8,128)S(1)} custom-call(s32[1]{0:T(128)} %bitcast.1.column_ref, bf16[256,1024]{1,0:T(8,128)(2,1)S(1)} %get-tuple-element.324.heads_ref, bf16[1024,8192]{1,0:T(8,128)(2,1)} %weight_ref.3, bf16[256,2048]{1,0:T(8,128)(2,1)S(1)} %copy-done, bf16[256,2048]{1,0:T(8,128)(2,1)S(1)} %collective-permute-done.144.refs_1_), custom_call_target="tpu_custom_call" | custom-call | flops 1 | bytes 1 | tf_op jit(solution)/shard_map/output_0/pallas_call | solution.py:525
  227.0 1.6 finish_1.1
  228.6 15.3 %collective-permute-done.147.refs_2_ = bf16[2,256,256]{2,1,0:T(8,128)(2,1)S(1)} collective-permute-done((bf16[2,256,256]{2,1,0:T(8,128)(2,1)S(1)}, bf16[2,256,256]{2,1,0:T(8,128)(2,1)S(1)}, u32[]{:S(2)}, u32[]{:S(2)}) %collective-permute-start.147) | collective-permute-done | bytes 262176 | tf_op jit(solution)/shard_map/ppermute | solution.py:699
  243.9 0.7 copy-done.6
  244.6 0.7 copy-done.7
  245.3 2.7 %pages.1 = bf16[16,64,256]{2,1,0:T(8,128)(2,1)} custom-call(s32[1]{0:T(128)} %bitcast.group_ref, s32[4]{0:T(128)} %counts_ref.3, s32[16]{0:T(128)} %destinations_ref.3, s32[64]{0:T(128)} %owner_ref.1, s32[16]{0:T(128)} %get-tuple-element.265.plan_ref, bf16[2,256,256]{2,1,0:T(8,128)(2,1)} %copy-done.4, bf16[2,256,256]{2,1,0:T(8,128)(2,1)} %copy-done.7, ...), custom_call_target="tpu_custom_call" | custom-call | flops 1 | bytes 1 | tf_op jit(solution)/shard_map/pages/pallas_call | solution.py:639
  (58 shorter events, 0.2 us)
Async XLA Ops:
  5.0 33.0 %collective-permute-start.16 = (bf16[256,2560]{1,0:T(8,128)(2,1)S(1)}, bf16[256,2560]{1,0:T(8,128)(2,1)}, u32[]{:S(2)}, u32[]{:S(2)}) collective-permute-start(bf16[256,2560]{1,0:T(8,128)(2,1)S(1)} %param.16), channel_id=1, source_target_pairs={{0,4},{12,8},{1,5},{13,9},{2,6},{14,10},{3,7},{15,11},{16,20},{28,... | collective-permute-start | bytes 3932168 | tf_op jit(solution)/shard_map/cond/branch_16_fun/ppermute | solution.py:707
  40.6 24.2 %collective-permute-start.30 = (bf16[256,2048]{1,0:T(8,128)(2,1)S(1)}, bf16[256,2048]{1,0:T(8,128)(2,1)}, u32[]{:S(2)}, u32[]{:S(2)}) collective-permute-start(bf16[256,2048]{1,0:T(8,128)(2,1)S(1)} %get-tuple-element.148), channel_id=1, source_target_pairs={{0,2},{1,3},{2,0},{3,1},{4,6},{5,7},{6,4},{7,5},{8,10},{9,11},{10,... | collective-permute-start | bytes 3145736 | tf_op jit(solution)/shard_map/cond/branch_1_fun/ppermute | solution.py:691
  42.2 32.4 %collective-permute-start.28 = (bf16[256,2560]{1,0:T(8,128)(2,1)S(1)}, bf16[256,2560]{1,0:T(8,128)(2,1)}, u32[]{:S(2)}, u32[]{:S(2)}) collective-permute-start(bf16[256,2560]{1,0:T(8,128)(2,1)S(1)} %get-tuple-element.147), channel_id=1, source_target_pairs={{0,8},{1,9},{2,10},{3,11},{16,24},{17,25},{18,26},{19,27}} | collective-permute-start | bytes 3932168 | tf_op jit(solution)/shard_map/cond/branch_1_fun/ppermute | solution.py:711
  48.8 16.0 %collective-permute-start.29 = (bf16[256,2048]{1,0:T(8,128)(2,1)S(1)}, bf16[256,2048]{1,0:T(8,128)(2,1)}, u32[]{:S(2)}, u32[]{:S(2)}) collective-permute-start(bf16[256,2048]{1,0:T(8,128)(2,1)S(1)} %get-tuple-element.148), channel_id=1, source_target_pairs={{0,1},{1,0},{2,3},{3,2},{4,5},{5,4},{6,7},{7,6},{8,9},{9,8},{10,11... | collective-permute-start | bytes 3145736 | tf_op jit(solution)/shard_map/cond/branch_1_fun/ppermute | solution.py:691
  64.8 9.8 %collective-permute-start.31 = (bf16[256,2048]{1,0:T(8,128)(2,1)}, bf16[256,2048]{1,0:T(8,128)(2,1)}, u32[]{:S(2)}, u32[]{:S(2)}) collective-permute-start(bf16[256,2048]{1,0:T(8,128)(2,1)} %collective-permute-done.30), channel_id=1, source_target_pairs={{0,1},{1,0},{2,3},{3,2},{4,5},{5,4},{6,7},{7,6},{8,9},{9,8},{10,11... | collective-permute-start | bytes 3145736 | tf_op jit(solution)/shard_map/cond/branch_1_fun/ppermute | solution.py:691
  74.6 5.0 %copy-start.13 = (bf16[256]{0:T(256)(128)(2,1)S(1)}, bf16[256]{0:T(256)(128)(2,1)}, u32[]{:S(2)}) copy-start(bf16[256]{0:T(256)(128)(2,1)} %param.72) | copy-start | bytes 1540
  74.6 5.0 %copy-start.10 = (bf16[8192]{0:T(1024)(128)(2,1)S(1)}, bf16[8192]{0:T(1024)(128)(2,1)}, u32[]{:S(2)}) copy-start(bf16[8192]{0:T(1024)(128)(2,1)} %param.68) | copy-start | bytes 49156
  74.6 5.0 %copy-start.3 = (s32[16]{0:T(128)S(1)}, s32[16]{0:T(128)}, u32[]{:S(2)}) copy-start(s32[16]{0:T(128)} %get-tuple-element.265.plan_ref) | copy-start | bytes 196
  78.4 13.6 %collective-permute-start.120 = (bf16[256,2048]{1,0:T(8,128)(2,1)}, bf16[256,2048]{1,0:T(8,128)(2,1)S(1)}, u32[]{:S(2)}, u32[]{:S(2)}) collective-permute-start(bf16[256,2048]{1,0:T(8,128)(2,1)} %get-tuple-element.308.refs_0_), channel_id=1, source_target_pairs={{0,1},{1,0},{2,3},{3,2},{4,5},{5,4},{6,7},{7,6},{8,9},{9,8},{10,11... | collective-permute-start | bytes 3145736 | tf_op jit(solution)/shard_map/ppermute | solution.py:691
  78.5 9.7 %collective-permute-start.124 = (bf16[512,128]{1,0:T(8,128)(2,1)}, bf16[512,128]{1,0:T(8,128)(2,1)S(1)}, u32[]{:S(2)}, u32[]{:S(2)}) collective-permute-start(bf16[512,128]{1,0:T(8,128)(2,1)} %get-tuple-element.292), channel_id=1, source_target_pairs={{0,1},{1,0},{2,3},{3,2},{4,5},{5,4},{6,7},{7,6},{8,9},{9,8},{10,11... | collective-permute-start | bytes 393224 | tf_op jit(solution)/shard_map/ppermute | solution.py:691
  79.0 9.2 %collective-permute-start.122 = (bf16[512,128]{1,0:T(8,128)(2,1)}, bf16[512,128]{1,0:T(8,128)(2,1)S(1)}, u32[]{:S(2)}, u32[]{:S(2)}) collective-permute-start(bf16[512,128]{1,0:T(8,128)(2,1)} %get-tuple-element.286), channel_id=1, source_target_pairs={{0,1},{1,0},{2,3},{3,2},{4,5},{5,4},{6,7},{7,6},{8,9},{9,8},{10,11... | collective-permute-start | bytes 393224 | tf_op jit(solution)/shard_map/ppermute | solution.py:691
  79.1 24.0 %collective-permute-start.121 = (bf16[128,2048]{1,0:T(8,128)(2,1)}, bf16[128,2048]{1,0:T(8,128)(2,1)S(1)}, u32[]{:S(2)}, u32[]{:S(2)}) collective-permute-start(bf16[128,2048]{1,0:T(8,128)(2,1)} %get-tuple-element.285), channel_id=1, source_target_pairs={{0,2},{1,3},{2,0},{3,1},{4,6},{5,7},{6,4},{7,5},{8,10},{9,11},{10,... | collective-permute-start | bytes 1572872 | tf_op jit(solution)/shard_map/ppermute | solution.py:691
  79.6 8.6 %copy-start.8 = (bf16[512,128]{1,0:T(8,128)(2,1)S(1)}, bf16[512,128]{1,0:T(8,128)(2,1)}, u32[]{:S(2)}) copy-start(bf16[512,128]{1,0:T(8,128)(2,1)} %get-tuple-element.291) | copy-start | bytes 393220
  79.6 8.6 %copy-start.9 = (bf16[512,128]{1,0:T(8,128)(2,1)S(1)}, bf16[512,128]{1,0:T(8,128)(2,1)}, u32[]{:S(2)}) copy-start(bf16[512,128]{1,0:T(8,128)(2,1)} %get-tuple-element.287) | copy-start | bytes 393220
  86.0 2.1 copy-start.1
  88.0 4.0 %copy-start.11 = (bf16[1024]{0:T(1024)(128)(2,1)S(1)}, bf16[1024]{0:T(1024)(128)(2,1)}, u32[]{:S(2)}) copy-start(bf16[1024]{0:T(1024)(128)(2,1)} %param.70) | copy-start | bytes 6148
  88.0 2.3 collective-permute-start.126
  88.3 14.8 %collective-permute-start.123 = (bf16[512,128]{1,0:T(8,128)(2,1)S(1)}, bf16[512,128]{1,0:T(8,128)(2,1)S(1)}, u32[]{:S(2)}, u32[]{:S(2)}) collective-permute-start(bf16[512,128]{1,0:T(8,128)(2,1)S(1)} %get-tuple-element.289), channel_id=1, source_target_pairs={{0,2},{1,3},{2,0},{3,1},{4,6},{5,7},{6,4},{7,5},{8,10},{9,11},{10,... | collective-permute-start | bytes 393224 | tf_op jit(solution)/shard_map/ppermute | solution.py:691
  89.9 13.2 %collective-permute-start.125 = (bf16[512,128]{1,0:T(8,128)(2,1)S(1)}, bf16[512,128]{1,0:T(8,128)(2,1)S(1)}, u32[]{:S(2)}, u32[]{:S(2)}) collective-permute-start(bf16[512,128]{1,0:T(8,128)(2,1)S(1)} %get-tuple-element.293), channel_id=1, source_target_pairs={{0,2},{1,3},{2,0},{3,1},{4,6},{5,7},{6,4},{7,5},{8,10},{9,11},{10,... | collective-permute-start | bytes 393224 | tf_op jit(solution)/shard_map/ppermute | solution.py:691
  90.4 12.7 %collective-permute-start.127 = (bf16[256,128]{1,0:T(8,128)(2,1)S(1)}, bf16[256,128]{1,0:T(8,128)(2,1)S(1)}, u32[]{:S(2)}, u32[]{:S(2)}) collective-permute-start(bf16[256,128]{1,0:T(8,128)(2,1)S(1)} %get-tuple-element.341), channel_id=1, source_target_pairs={{0,2},{1,3},{2,0},{3,1},{4,6},{5,7},{6,4},{7,5},{8,10},{9,11},{10,... | collective-permute-start | bytes 196616 | tf_op jit(solution)/shard_map/ppermute | solution.py:691
  92.0 2.2 copy-start.2
  94.2 8.3 %copy-start.12 = (bf16[128,2048]{1,0:T(8,128)(2,1)S(1)}, bf16[128,2048]{1,0:T(8,128)(2,1)}, u32[]{:S(2)}) copy-start(bf16[128,2048]{1,0:T(8,128)(2,1)} %get-tuple-element.302) | copy-start | bytes 1572868
  102.5 13.4 %collective-permute-start.128 = (bf16[128,2048]{1,0:T(8,128)(2,1)S(1)}, bf16[128,2048]{1,0:T(8,128)(2,1)S(1)}, u32[]{:S(2)}, u32[]{:S(2)}) collective-permute-start(bf16[128,2048]{1,0:T(8,128)(2,1)S(1)} %copy-done.12), channel_id=1, source_target_pairs={{0,2},{1,3},{2,0},{3,1},{4,6},{5,7},{6,4},{7,5},{8,10},{9,11},{10,... | collective-permute-start | bytes 1572872 | tf_op jit(solution)/shard_map/ppermute | solution.py:691
  112.2 10.2 %copy-start = (bf16[256,2048]{1,0:T(8,128)(2,1)S(1)}, bf16[256,2048]{1,0:T(8,128)(2,1)}, u32[]{:S(2)}) copy-start(bf16[256,2048]{1,0:T(8,128)(2,1)} %get-tuple-element.308.refs_0_) | copy-start | bytes 3145732
  115.9 1.5 collective-permute-start.129
  115.9 14.2 %collective-permute-start.135 = (bf16[256,2048]{1,0:T(8,128)(2,1)S(1)}, bf16[256,2048]{1,0:T(8,128)(2,1)S(1)}, u32[]{:S(2)}, u32[]{:S(2)}) collective-permute-start(bf16[256,2048]{1,0:T(8,128)(2,1)S(1)} %get-tuple-element.310), channel_id=1, source_target_pairs={{0,1},{1,0},{2,3},{3,2},{4,5},{5,4},{6,7},{7,6},{8,9},{9,8},{10,11... | collective-permute-start | bytes 3145736 | tf_op jit(solution)/shard_map/ppermute | solution.py:691
  116.4 2.9 %collective-permute-start.130 = (bf16[64,2048]{1,0:T(8,128)(2,1)S(1)}, bf16[64,2048]{1,0:T(8,128)(2,1)S(1)}, u32[]{:S(2)}, u32[]{:S(2)}) collective-permute-start(bf16[64,2048]{1,0:T(8,128)(2,1)S(1)} %get-tuple-element.304), channel_id=1, source_target_pairs={{0,1},{1,0},{2,3},{3,2},{4,5},{5,4},{6,7},{7,6},{8,9},{9,8},{10,11... | collective-permute-start | bytes 786440 | tf_op jit(solution)/shard_map/ppermute | solution.py:691
  116.4 6.0 %collective-permute-start.133 = (bf16[128,2048]{1,0:T(8,128)(2,1)S(1)}, bf16[128,2048]{1,0:T(8,128)(2,1)S(1)}, u32[]{:S(2)}, u32[]{:S(2)}) collective-permute-start(bf16[128,2048]{1,0:T(8,128)(2,1)S(1)} %collective-permute-done.121.refs_2_), channel_id=1, source_target_pairs={{0,1},{1,0},{2,3},{3,2},{4,5},{5,4},{6,7},{7,6},{8,9},{9,8},{10,11... | collective-permute-start | bytes 1572872 | tf_op jit(solution)/shard_map/ppermute | solution.py:691
  116.9 5.5 %collective-permute-start.134 = (bf16[128,2048]{1,0:T(8,128)(2,1)S(1)}, bf16[128,2048]{1,0:T(8,128)(2,1)S(1)}, u32[]{:S(2)}, u32[]{:S(2)}) collective-permute-start(bf16[128,2048]{1,0:T(8,128)(2,1)S(1)} %collective-permute-done.128.refs_3_), channel_id=1, source_target_pairs={{0,1},{1,0},{2,3},{3,2},{4,5},{5,4},{6,7},{7,6},{8,9},{9,8},{10,11... | collective-permute-start | bytes 1572872 | tf_op jit(solution)/shard_map/ppermute | solution.py:691
  117.4 3.7 %collective-permute-start.131 = (bf16[64,2048]{1,0:T(8,128)(2,1)S(1)}, bf16[64,2048]{1,0:T(8,128)(2,1)S(1)}, u32[]{:S(2)}, u32[]{:S(2)}) collective-permute-start(bf16[64,2048]{1,0:T(8,128)(2,1)S(1)} %get-tuple-element.305), channel_id=1, source_target_pairs={{0,1},{1,0},{2,3},{3,2},{4,5},{5,4},{6,7},{7,6},{8,9},{9,8},{10,11... | collective-permute-start | bytes 786440 | tf_op jit(solution)/shard_map/ppermute | solution.py:691
  119.3 2.2 collective-permute-start.132
  121.8 16.6 %collective-permute-start.136 = (bf16[128,2048]{1,0:T(8,128)(2,1)S(1)}, bf16[128,2048]{1,0:T(8,128)(2,1)S(1)}, u32[]{:S(2)}, u32[]{:S(2)}) collective-permute-start(bf16[128,2048]{1,0:T(8,128)(2,1)S(1)} %get-tuple-element.307), channel_id=1, source_target_pairs={{0,2},{1,3},{2,0},{3,1},{4,6},{5,7},{6,4},{7,5},{8,10},{9,11},{10,... | collective-permute-start | bytes 1572872 | tf_op jit(solution)/shard_map/ppermute | solution.py:691
  127.1 1.3 collective-permute-start.137
  128.5 9.9 %collective-permute-start.138 = (bf16[256,128]{1,0:T(8,128)(2,1)S(1)}, bf16[256,128]{1,0:T(8,128)(2,1)S(1)}, u32[]{:S(2)}, u32[]{:S(2)}) collective-permute-start(bf16[256,128]{1,0:T(8,128)(2,1)S(1)} %get-tuple-element.339), channel_id=1, source_target_pairs={{0,2},{1,3},{2,0},{3,1},{4,6},{5,7},{6,4},{7,5},{8,10},{9,11},{10,... | collective-permute-start | bytes 196616 | tf_op jit(solution)/shard_map/ppermute | solution.py:691
  143.1 13.8 %collective-permute-start.143 = (bf16[128,2048]{1,0:T(8,128)(2,1)S(1)}, bf16[128,2048]{1,0:T(8,128)(2,1)S(1)}, u32[]{:S(2)}, u32[]{:S(2)}) collective-permute-start(bf16[128,2048]{1,0:T(8,128)(2,1)S(1)} %get-tuple-element.322), channel_id=1, source_target_pairs={{0,2},{1,3},{2,0},{3,1},{4,6},{5,7},{6,4},{7,5},{8,10},{9,11},{10,... | collective-permute-start | bytes 1572872 | tf_op jit(solution)/shard_map/ppermute | solution.py:691
  143.7 5.5 %collective-permute-start.139 = (bf16[64,2048]{1,0:T(8,128)(2,1)S(1)}, bf16[64,2048]{1,0:T(8,128)(2,1)S(1)}, u32[]{:S(2)}, u32[]{:S(2)}) collective-permute-start(bf16[64,2048]{1,0:T(8,128)(2,1)S(1)} %get-tuple-element.317), channel_id=1, source_target_pairs={{0,1},{1,0},{2,3},{3,2},{4,5},{5,4},{6,7},{7,6},{8,9},{9,8},{10,11... | collective-permute-start | bytes 786440 | tf_op jit(solution)/shard_map/ppermute | solution.py:691
  143.7 5.5 %collective-permute-start.140 = (bf16[64,2048]{1,0:T(8,128)(2,1)S(1)}, bf16[64,2048]{1,0:T(8,128)(2,1)S(1)}, u32[]{:S(2)}, u32[]{:S(2)}) collective-permute-start(bf16[64,2048]{1,0:T(8,128)(2,1)S(1)} %get-tuple-element.318), channel_id=1, source_target_pairs={{0,1},{1,0},{2,3},{3,2},{4,5},{5,4},{6,7},{7,6},{8,9},{9,8},{10,11... | collective-permute-start | bytes 786440 | tf_op jit(solution)/shard_map/ppermute | solution.py:691
  144.2 5.0 %collective-permute-start.141 = (bf16[64,2048]{1,0:T(8,128)(2,1)S(1)}, bf16[64,2048]{1,0:T(8,128)(2,1)S(1)}, u32[]{:S(2)}, u32[]{:S(2)}) collective-permute-start(bf16[64,2048]{1,0:T(8,128)(2,1)S(1)} %get-tuple-element.319), channel_id=1, source_target_pairs={{0,1},{1,0},{2,3},{3,2},{4,5},{5,4},{6,7},{7,6},{8,9},{9,8},{10,11... | collective-permute-start | bytes 786440 | tf_op jit(solution)/shard_map/ppermute | solution.py:691
  144.2 5.0 %collective-permute-start.142 = (bf16[64,2048]{1,0:T(8,128)(2,1)S(1)}, bf16[64,2048]{1,0:T(8,128)(2,1)S(1)}, u32[]{:S(2)}, u32[]{:S(2)}) collective-permute-start(bf16[64,2048]{1,0:T(8,128)(2,1)S(1)} %get-tuple-element.320), channel_id=1, source_target_pairs={{0,1},{1,0},{2,3},{3,2},{4,5},{5,4},{6,7},{7,6},{8,9},{9,8},{10,11... | collective-permute-start | bytes 786440 | tf_op jit(solution)/shard_map/ppermute | solution.py:691
  156.9 67.0 %collective-permute-start.144 = (bf16[256,2048]{1,0:T(8,128)(2,1)S(1)}, bf16[256,2048]{1,0:T(8,128)(2,1)S(1)}, u32[]{:S(2)}, u32[]{:S(2)}) collective-permute-start(bf16[256,2048]{1,0:T(8,128)(2,1)S(1)} %get-tuple-element.326), channel_id=1, source_target_pairs={{0,1},{1,0},{2,3},{3,2},{4,5},{5,4},{6,7},{7,6},{8,9},{9,8},{10,11... | collective-permute-start | bytes 3145736 | tf_op jit(solution)/shard_map/ppermute | solution.py:691
  156.9 70.1 %collective-permute-start.145 = (bf16[256,2048]{1,0:T(8,128)(2,1)S(1)}, bf16[256,2048]{1,0:T(8,128)(2,1)S(1)}, u32[]{:S(2)}, u32[]{:S(2)}) collective-permute-start(bf16[256,2048]{1,0:T(8,128)(2,1)S(1)} %add.3), channel_id=1, source_target_pairs={{0,2},{1,3},{2,0},{3,1},{4,6},{5,7},{6,4},{7,5},{8,10},{9,11},{10,... | collective-permute-start | bytes 3145736 | tf_op jit(solution)/shard_map/ppermute | solution.py:691
  157.4 66.4 %copy-start.4 = (bf16[2,256,256]{2,1,0:T(8,128)(2,1)}, bf16[2,256,256]{2,1,0:T(8,128)(2,1)S(1)}, u32[]{:S(2)}) copy-start(bf16[2,256,256]{2,1,0:T(8,128)(2,1)S(1)} %pad_maximum_fusion.refs_0_) | copy-start | bytes 786436
  157.4 71.2 %collective-permute-start.148 = (bf16[2,256,256]{2,1,0:T(8,128)(2,1)S(1)}, bf16[2,256,256]{2,1,0:T(8,128)(2,1)S(1)}, u32[]{:S(2)}, u32[]{:S(2)}) collective-permute-start(bf16[2,256,256]{2,1,0:T(8,128)(2,1)S(1)} %pad_maximum_fusion.refs_0_), channel_id=1, source_target_pairs={{0,12},{4,0},{8,4},{12,8},{1,13},{5,1},{9,5},{13,9},{2,14},{6,2},{... | collective-permute-start | bytes 786440 | tf_op jit(solution)/shard_map/ppermute | solution.py:699
  217.6 26.3 %collective-permute-start.147 = (bf16[2,256,256]{2,1,0:T(8,128)(2,1)S(1)}, bf16[2,256,256]{2,1,0:T(8,128)(2,1)S(1)}, u32[]{:S(2)}, u32[]{:S(2)}) collective-permute-start(bf16[2,256,256]{2,1,0:T(8,128)(2,1)S(1)} %pad_maximum_fusion.refs_0_), channel_id=1, source_target_pairs={{0,8},{4,12},{8,0},{12,4},{1,9},{5,13},{9,1},{13,5},{2,10},{6,14},... | collective-permute-start | bytes 786440 | tf_op jit(solution)/shard_map/ppermute | solution.py:699
  220.4 23.5 %collective-permute-start.146 = (bf16[2,256,256]{2,1,0:T(8,128)(2,1)S(1)}, bf16[2,256,256]{2,1,0:T(8,128)(2,1)S(1)}, u32[]{:S(2)}, u32[]{:S(2)}) collective-permute-start(bf16[2,256,256]{2,1,0:T(8,128)(2,1)S(1)} %pad_maximum_fusion.refs_0_), channel_id=1, source_target_pairs={{0,4},{4,8},{8,12},{12,0},{1,5},{5,9},{9,13},{13,1},{2,6},{6,10},{... | collective-permute-start | bytes 786440 | tf_op jit(solution)/shard_map/ppermute | solution.py:699
  228.6 15.3 %copy-start.5 = (bf16[2,256,256]{2,1,0:T(8,128)(2,1)}, bf16[2,256,256]{2,1,0:T(8,128)(2,1)S(1)}, u32[]{:S(2)}) copy-start(bf16[2,256,256]{2,1,0:T(8,128)(2,1)S(1)} %collective-permute-done.148.refs_3_) | copy-start | bytes 786436
  243.9 0.7 copy-start.6
  244.6 0.7 copy-start.7
